TPU v7x, 32 devices: a whole 2x2x4 slice. The times are simulated.
32 devices in a mesh: dp: 2 (over y), expert: 16 (over z, x, core).
Axes of the slice: x: 2, y: 2, z: 4, core: 2. Of those that a mesh axis runs over, the one named last changes fastest.
Arguments:
- hidden_rows: bfloat16 [768, 4096], P(None, ('dp', 'expert')), may hold values from -6 to 6
- grad_rows: bfloat16 [4096, 2560], P(('dp', 'expert')), may hold values from -0.1796875 to 0.1796875
- block_slot: int32 [32, 1], P(('dp', 'expert')), may hold values from 0 to 1
- live_rows: int32 [32], P(('dp', 'expert')), may hold values from 16 to 128
- replica_plan: int32 [16], replicated, may hold values from 0 to 3
- master: float32 [16, 768, 640], P('expert', 'dp'), may hold values from -0.21875 to 0.21875
- moment_one: float32 [16, 768, 640], P('expert', 'dp'), may hold values from -1.8 to 1.8
- moment_two: float32 [16, 768, 640], P('expert', 'dp'), may hold values from 0.01 to 1
Outputs:
- master_new: float32 [16, 768, 640], P('expert', 'dp')
- first_new: float32 [16, 768, 640], P('expert', 'dp')
- second_new: float32 [16, 768, 640], P('expert', 'dp')
- replica_weight: bfloat16 [16, 768, 2560], P('expert', 'dp')
Inputs may be any that keep to these rules, and one draw needn't show every extreme that they name: replica_plan[j] is the expert of which the devices at index j along the expert axis host a replica; it may equal j mod 4. `block_slot`: 0 marks a block of the primary expert, 1 a block of the replica.
All inputs are finite; a program needn't handle non-finite values.
Results may differ from a plain program's by a relative error of at most 0.001.
Values may be sent and summed in bfloat16 or wider, within the bound.
No kernel may reach another device: no remote copies, remote signals or barrier semaphores. Data moves between devices by JAX's collectives and lax.ppermute only.
A program may use at most 64 MiB of HBM per device.

v0:
```python
import functools

import jax
import jax.numpy as jnp
from jax import lax
from jax.experimental import pallas as pl
from jax.experimental.pallas import tpu as pltpu
from jax.sharding import PartitionSpec as P

QUART = 4
LANES = 128
META_ROWS = 16


beta_one = 0.9
beta_two = 0.95
learn_rate = 0.01
decay_rate = 0.1
epsilon = 1e-08
step_count = 10.0

VMEM = pl.BlockSpec(memory_space=pltpu.VMEM)
SMEM = pl.BlockSpec(memory_space=pltpu.SMEM)
ANYWHERE = pl.BlockSpec(memory_space=pl.ANY)


def vmem_for(*arrays):
    return int(sum(a.size * a.dtype.itemsize for a in arrays) * 5 // 4) + (8 << 20)


def call(kernel, out_shapes, scalars, arrays, flops=0):
    moved = sum(a.size * a.dtype.itemsize for a in (*arrays, *out_shapes))
    return pl.pallas_call(
        kernel,
        out_shape=tuple(out_shapes),
        in_specs=[SMEM] * len(scalars) + [VMEM] * len(arrays),
        out_specs=tuple([VMEM] * len(out_shapes)),
        compiler_params=pltpu.CompilerParams(vmem_limit_bytes=vmem_for(*arrays, *out_shapes)),
        cost_estimate=pl.CostEstimate(flops=flops // 64, bytes_accessed=moved // 64, transcendentals=0),
    )(*scalars, *arrays)


def from_behind(block, axis, distance):
    devices = range(lax.axis_size(axis))
    route = [((i - distance) % len(devices), i) for i in devices]
    return lax.ppermute(block, axis, route)


def from_mate(block, axis, bit):
    return lax.ppermute(block, axis, [(i ^ bit, i) for i in range(lax.axis_size(axis))])


def gather_mates(block, axis, count, least=1):
    held = {0: block}
    bit = count // 2
    while bit >= least:
        held.update({m | bit: from_mate(held[m], axis, bit) for m in list(held)})
        bit //= 2
    return [held.get(m) for m in range(count)]


def after(value, *others):
    return lax.optimization_barrier((value, *others))[0] if others else value


def exchange(packs, bit):
    keys = [(step, mate | bit) for pack, _ in packs for step, mate in pack]
    blocks = [block for _, block in packs]
    return keys, from_mate(jnp.concatenate(blocks) if len(blocks) > 1 else blocks[0], "expert", bit)


def places(packs, first):
    found = {}
    for at, (keys, block) in enumerate(packs):
        rows = block.shape[0] // len(keys)
        found.update({key: (first + at, i * rows) for i, key in enumerate(keys)})
    return found


def place(owner_count):
    own = lax.axis_index("expert")
    return own // owner_count, own % owner_count


def message_kernel(owner_count, slot_ref, live_ref, hidden_hbm, grad_hbm, *refs):
    *message_refs, hidden_ref, grad_ref, sems = refs
    loads = [
        pltpu.make_async_copy(hidden_hbm, hidden_ref, sems.at[0]),
        pltpu.make_async_copy(grad_hbm, grad_ref, sems.at[1]),
    ]
    for load in loads:
        load.start()
    for load in loads:
        load.wait()
    own_block, _ = place(owner_count)
    hidden_units, tok_rows = hidden_ref.shape
    block_width = grad_ref.shape[1] // QUART
    parts = block_width // LANES
    live = live_ref[0]
    slot = slot_ref[0, 0]
    kept = lax.broadcasted_iota(jnp.int32, (tok_rows, LANES), 0) < live
    meta = jnp.full((META_ROWS, LANES), slot.astype(jnp.float32)).astype(jnp.bfloat16)

    for step, message in enumerate(message_refs):
        target = lax.rem(own_block + step, QUART)
        for part in range(parts):
            start = pl.multiple_of(target * block_width + part * LANES, LANES)
            columns = grad_ref[:, pl.ds(start, LANES)].astype(jnp.float32)
            row = part * tok_rows
            message[row : row + tok_rows, :] = jnp.where(kept, columns, 0.0).astype(jnp.bfloat16)
        row = parts * tok_rows
        message[row : row + META_ROWS, :] = meta
        message[row + META_ROWS :, :] = hidden_ref[...]


def partial_kernel(owner_count, tok_rows, share_rows, where, base, steps, plan_ref, *refs):
    totals = refs[-len(steps) :]
    own_block, own_expert = place(owner_count)
    group, groups = lax.axis_index("dp"), lax.axis_size("dp")
    rows, block_width = totals[0].shape
    parts = block_width // LANES
    chunk = next(c for c in (208, 192, 176, 128, 112, 96, 64, 48, 32, 16) if rows % c == 0)
    bits = []
    for first in range(0, len(where), 16):
        packed = jnp.zeros((META_ROWS, LANES), jnp.float32)
        for at, (_, (ref, row)) in enumerate(where[first : first + 16]):
            meta = refs[ref][row + parts * tok_rows : row + parts * tok_rows + META_ROWS, :]
            packed = packed + meta.astype(jnp.float32) * float(1 << at)
        bits.append(jnp.max(packed).astype(jnp.int32))
    for total in totals:
        total[...] = jnp.zeros_like(total)
    for at, ((step, mate), (ref, row)) in enumerate(where):
        source_expert = own_expert ^ mate
        source = lax.rem(own_block + QUART - step, QUART) * owner_count + source_expert
        is_replica = ((bits[at // 16] >> (at % 16)) & 1) == 1
        target = jnp.where(is_replica, plan_ref[source], source_expert)

        @pl.when(target == own_expert)
        def _():
            columns = jnp.concatenate(
                [refs[ref][row + p * tok_rows : row + (p + 1) * tok_rows, :] for p in range(parts)],
                axis=1,
            )
            for total, ahead in zip(totals, steps):
                start = row + base + lax.rem(group + ahead, groups) * share_rows

                @pl.loop(0, rows // chunk)
                def _(i):
                    term = jnp.dot(
                        refs[ref][pl.ds(pl.multiple_of(start + i * chunk, 16), chunk), :],
                        columns,
                        preferred_element_type=jnp.float32,
                    )
                    rounded = term.astype(jnp.bfloat16).astype(jnp.float32)
                    into = pl.ds(pl.multiple_of(i * chunk, 16), chunk)
                    total[into, :] += jnp.where(is_replica, rounded, term)


def update_kernel(parts, held, span, pieces, *refs):
    terms, (master, one, two) = refs[:parts], refs[parts : parts + 3]
    *outs, fresh, new_rows, sems = refs[parts + 3 + held :]
    first, _ = span
    copies = []
    for at, (start, size) in enumerate(pieces):
        inside, placed = pl.ds(start, size), pl.ds(first + start, size)
        gradient = terms[0][inside, :]
        for term in terms[1:]:
            gradient = gradient + term[inside, :]
        weights = master[placed, :]
        first_next = beta_one * one[placed, :] + (1.0 - beta_one) * gradient
        second_next = beta_two * two[placed, :] + (1.0 - beta_two) * gradient * gradient
        scaled_first = first_next / (1.0 - beta_one**step_count)
        scaled_second = second_next / (1.0 - beta_two**step_count)
        direction = scaled_first / (jnp.sqrt(scaled_second) + epsilon)
        weights_next = weights - learn_rate * (direction + decay_rate * weights)
        fresh[inside, :] = weights_next.astype(jnp.bfloat16)
        for which, value in enumerate((weights_next, first_next, second_next)):
            new_rows[which, inside, :] = value
            copies.append(
                pltpu.make_async_copy(
                    new_rows.at[which, inside, :], outs[which].at[placed, :], sems.at[which, at]
                )
            )
            copies[-1].start()
    for copy in copies:
        copy.wait()


def update(terms, states, span, held):
    length = span[1]
    rows, width = states[0].shape
    pieces = [(start, min(64, length - start)) for start in range(0, length, 64)]
    whole = jax.ShapeDtypeStruct((rows, width), jnp.float32)
    inputs = len(terms) + len(states)
    return pl.pallas_call(
        functools.partial(update_kernel, len(terms), len(held), span, pieces),
        out_shape=(whole, whole, whole, jax.ShapeDtypeStruct((length, width), jnp.bfloat16)),
        in_specs=[VMEM] * inputs + [ANYWHERE] * len(held),
        out_specs=(ANYWHERE, ANYWHERE, ANYWHERE, VMEM),
        scratch_shapes=[
            pltpu.VMEM((3, length, width), jnp.float32),
            pltpu.SemaphoreType.DMA((3, len(pieces))),
        ],
        input_output_aliases={inputs + i: i for i in range(len(held))},
        compiler_params=pltpu.CompilerParams(vmem_limit_bytes=24 << 20),
        cost_estimate=pl.CostEstimate(
            flops=length * width, bytes_accessed=length * width, transcendentals=0
        ),
    )(*terms, *states, *held)


def choose_kernel(owner_count, plan_ref, *refs):
    candidates, chosen = refs[:owner_count], refs[owner_count:]
    own_block, own_expert = place(owner_count)
    for step, out in enumerate(chosen):
        wanted = plan_ref[lax.rem(own_block + step, QUART) * owner_count + own_expert]
        for mate, candidate in enumerate(candidates):

            @pl.when(wanted == own_expert ^ mate)
            def _():
                out[...] = candidate[...]


def offer_kernel(owner_count, plan_ref, *refs):
    held, out = refs[:-1], refs[-1]
    own_block, own_expert = place(owner_count)
    wanted = plan_ref[own_block * owner_count + (own_expert ^ 1)]
    half = owner_count // 2
    rows = held[0].shape[0]
    for pair in range(half):

        @pl.when((wanted ^ own_expert) >> 1 == pair)
        def _():
            out[0] = held[pair][...]
            for step in range(1, QUART):
                out[step] = held[half + pair][(step - 1) * rows : step * rows, :]


def assemble_kernel(owner_count, span, later, plan_ref, *refs):
    *blocks, out, sems = refs
    own_block, own_expert = place(owner_count)
    apart = plan_ref[own_block * owner_count + own_expert] ^ own_expert
    first, rows = span
    half = owner_count // 2

    def put(sources, start):
        copies = []
        for step, source in enumerate(sources):
            width = source.shape[1]
            column = pl.multiple_of(lax.rem(own_block + QUART - step, QUART) * width, LANES)
            target = out.at[pl.ds(start, source.shape[0]), pl.ds(column, width)]
            copies.append(pltpu.make_async_copy(source, target, sems.at[step]))
            copies[-1].start()
        for copy in copies:
            copy.wait()

    if later:
        offered, _ = blocks

        @pl.when(apart & 1 == 1)
        def _():
            put([offered.at[step] for step in range(QUART)], first)

        return

    near, far, received = blocks[:half], blocks[half : 2 * half], blocks[2 * half :]
    put(received, first + rows)
    for pair in range(half):

        @pl.when(apart == 2 * pair)
        def _():
            sources = [far[pair].at[pl.ds(step * rows, rows), :] for step in range(QUART - 1)]
            put([near[pair], *sources], first)


def assemble(owner_count, span, plan, blocks, shape, held=None):
    later = held is not None
    inputs = [*blocks, held] if later else blocks
    return pl.pallas_call(
        functools.partial(assemble_kernel, owner_count, span, later),
        out_shape=shape,
        in_specs=[SMEM] + [VMEM] * len(blocks) + [ANYWHERE] * later,
        out_specs=ANYWHERE,
        scratch_shapes=[pltpu.SemaphoreType.DMA((QUART,))],
        input_output_aliases={1 + len(blocks): 0} if later else {},
        compiler_params=pltpu.CompilerParams(vmem_limit_bytes=vmem_for(*blocks)),
        cost_estimate=pl.CostEstimate(flops=1, bytes_accessed=1 << 14, transcendentals=0),
    )(plan, *inputs)


def per_device(
    hidden_rows, grad_rows, block_slot, live_rows, replica_plan, master, moment_one, moment_two
):
    owner_count = lax.axis_size("expert") // QUART
    groups = lax.axis_size("dp")
    hidden_units, tok_rows = hidden_rows.shape
    block_width = grad_rows.shape[1] // QUART
    share_rows = hidden_units // groups
    assert block_slot.shape[1] == 1 and tok_rows == LANES and block_width % LANES == 0
    shape = jax.ShapeDtypeStruct
    lead = share_rows * 13 // 24 // 16 * 16
    spans = ((0, lead), (lead, share_rows - lead))

    head_rows = (block_width // LANES) * tok_rows + META_ROWS
    outs = [shape((head_rows + hidden_units, LANES), jnp.bfloat16)] * QUART
    messages = pl.pallas_call(
        functools.partial(message_kernel, owner_count),
        out_shape=tuple(outs),
        in_specs=[SMEM, SMEM, ANYWHERE, ANYWHERE],
        out_specs=tuple([VMEM] * len(outs)),
        scratch_shapes=[
            pltpu.VMEM(hidden_rows.shape, hidden_rows.dtype),
            pltpu.VMEM(grad_rows.shape, grad_rows.dtype),
            pltpu.SemaphoreType.DMA((2,)),
        ],
        compiler_params=pltpu.CompilerParams(
            vmem_limit_bytes=vmem_for(hidden_rows, grad_rows, *outs)
        ),
        cost_estimate=pl.CostEstimate(flops=1, bytes_accessed=1 << 14, transcendentals=0),
    )(block_slot, live_rows, hidden_rows, grad_rows)

    def across(block, step):
        return from_behind(block, "expert", step * owner_count) if step else block

    first_bit = owner_count // 2
    other_bits = [1 << i for i in reversed(range(first_bit.bit_length() - 1))]
    own = [([(0, 0)], messages[0])]
    sides = [([(step, 0)], across(messages[step], step)) for step in (1, 3)]
    own += [exchange(own, first_bit)]
    last = across(after(messages[2], *(block for _, block in sides)), 2)
    crossed = [exchange(sides, first_bit)]
    own += sides
    for bit in other_bits:
        own += [exchange(own, bit)]
    last = [([(2, 0)], last)]
    last += [exchange(last, first_bit)]
    last = crossed + last
    for bit in other_bits:
        last += [exchange(last, bit)]
    heads = own + last
    head_at = places(heads, 0)

    def partials(at, steps, wait_for):
        first, rows = spans[at]
        return call(
            functools.partial(
                partial_kernel,
                owner_count,
                tok_rows,
                share_rows,
                tuple(head_at.items()),
                head_rows + first,
                steps,
            ),
            [shape((rows, block_width), jnp.float32)] * len(steps),
            (after(replica_plan, *wait_for),),
            [block for _, block in heads],
            2 * len(steps) * rows * tok_rows * block_width * QUART,
        )

    states = (master[0], moment_one[0], moment_two[0])
    ahead = tuple(range(1, groups))
    block = lambda rows: shape((rows, block_width), jnp.bfloat16)

    far_one = partials(0, ahead, ())
    came_one = [from_behind(p, "dp", step) for step, p in zip(ahead, far_one)]
    near_one = partials(0, (0,), far_one)
    far_two = partials(1, ahead, near_one)
    near_two = partials(1, (0,), far_two)
    came_one = [after(term, *near_two) for term in came_one]
    came_two = [
        from_behind(after(p, *came_one), "dp", step) for step, p in zip(ahead, far_two)
    ]
    *held, fresh_one = update((*near_one, *came_one), states, spans[0], ())

    lines = [across(fresh_one, step) for step in range(QUART)]

    came_two = [after(term, fresh_one) for term in came_two]
    *held, fresh_two = update((*near_two, *came_two), states, spans[1], held)

    mates_two = gather_mates(fresh_two, "expert", owner_count)
    near_wide = gather_mates(fresh_one, "expert", owner_count, 2)[::2]
    crossed = mates_two[owner_count // 2], near_wide[-1]
    lines[1:] = [after(line, *crossed) for line in lines[1:]]
    chosen = call(
        functools.partial(choose_kernel, owner_count),
        [block(spans[1][1])] * QUART,
        (after(replica_plan, *lines),),
        mates_two,
    )
    received = [across(c, step) for step, c in enumerate(chosen)]

    stacked = jnp.concatenate(lines[1:])
    far_wide = gather_mates(stacked, "expert", owner_count, 2)[::2]
    (offer,) = call(
        functools.partial(offer_kernel, owner_count),
        [shape((QUART, spans[0][1], block_width), jnp.bfloat16)],
        (after(replica_plan, *received[1:]),),
        (*near_wide, *far_wide),
    )
    result = shape((share_rows, QUART * block_width), jnp.bfloat16)
    placed = assemble(
        owner_count, spans[0], replica_plan, [*near_wide, *far_wide, *received], result
    )
    offer = from_mate(offer, "expert", 1)
    replica_weight = assemble(owner_count, spans[0], replica_plan, [offer], result, placed)
    return (*(state[None] for state in held), replica_weight[None])


def solution(mesh):
    return jax.shard_map(
        per_device,
        mesh=mesh,
        in_specs=(
            P(None, ("dp", "expert")),
            P(("dp", "expert"), None),
            P(("dp", "expert"), None),
            P(("dp", "expert")),
            P(),
            P("expert", "dp", None),
            P("expert", "dp", None),
            P("expert", "dp", None),
        ),
        out_specs=(
            P("expert", "dp", None),
            P("expert", "dp", None),
            P("expert", "dp", None),
            P("expert", "dp", None),
        ),
        check_vma=False,
    )
```

profile of v0, /device:TPU:9, one launch (start us, length us, event | category | flops | bytes accessed | tf_op | source)
XLA Modules:
  0.0 128.3 jit_solution(13069802357861006668)
XLA Ops:
  1.9 1.1 copy-done.3
  3.0 0.9 copy-done.4
  3.9 0.6 shard_map.111
  4.5 1.4 %collective-permute-start.1 = (bf16[1424,128]{1,0:T(8,128)(2,1)S(1)}, bf16[1424,128]{1,0:T(8,128)(2,1)S(1)}, u32[]{:S(2)}, u32[]{:S(2)}) collective-permute-start(bf16[1424,128]{1,0:T(8,128)(2,1)S(1)} %get-tuple-element.33), channel_id=1, source_target_pairs={{12,0},{13,1},{14,2},{15,3},{0,4},{1,5},{2,6},{3,7},{4,8},{5,9},{6... | collective-permute-start | bytes 1093640 | tf_op jit(solution)/shard_map/ppermute | solution.py:46
  5.9 0.2 collective-permute-start.2
  6.1 1.2 collective-permute-start
  7.3 6.7 %collective-permute-done.1.refs_2_ = bf16[1424,128]{1,0:T(8,128)(2,1)S(1)} collective-permute-done((bf16[1424,128]{1,0:T(8,128)(2,1)S(1)}, bf16[1424,128]{1,0:T(8,128)(2,1)S(1)}, u32[]{:S(2)}, u32[]{:S(2)}) %collective-permute-start.1) | collective-permute-done | bytes 364576 | tf_op jit(solution)/shard_map/ppermute | solution.py:46
  14.0 9.7 %collective-permute-done.2.refs_3_ = bf16[1424,128]{1,0:T(8,128)(2,1)S(1)} collective-permute-done((bf16[1424,128]{1,0:T(8,128)(2,1)S(1)}, bf16[1424,128]{1,0:T(8,128)(2,1)S(1)}, u32[]{:S(2)}, u32[]{:S(2)}) %collective-permute-start.2) | collective-permute-done | bytes 364576 | tf_op jit(solution)/shard_map/ppermute | solution.py:46
  23.7 0.2 collective-permute-start.5
  23.9 1.3 collective-permute-start.4
  25.2 14.4 %collective-permute-done.5.refs_6_ = bf16[1424,128]{1,0:T(8,128)(2,1)S(1)} collective-permute-done((bf16[1424,128]{1,0:T(8,128)(2,1)S(1)}, bf16[1424,128]{1,0:T(8,128)(2,1)S(1)}, u32[]{:S(2)}, u32[]{:S(2)}) %collective-permute-start.5) | collective-permute-done | bytes 364576 | tf_op jit(solution)/shard_map/ppermute | solution.py:46
  39.6 1.5 %collective-permute-start.6 = (bf16[1424,128]{1,0:T(8,128)(2,1)S(1)}, bf16[1424,128]{1,0:T(8,128)(2,1)S(1)}, u32[]{:S(2)}, u32[]{:S(2)}) collective-permute-start(bf16[1424,128]{1,0:T(8,128)(2,1)S(1)} %collective-permute-done.5.refs_6_), channel_id=1, source_target_pairs={{2,0},{3,1},{0,2},{1,3},{6,4},{7,5},{4,6},{5,7},{10,8},{11,9},{8,1... | collective-permute-start | bytes 1093640 | tf_op jit(solution)/shard_map/ppermute | solution.py:50
  41.2 0.9 collective-permute-start.3
  42.1 6.8 %collective-permute-done.6.refs_7_ = bf16[1424,128]{1,0:T(8,128)(2,1)S(1)} collective-permute-done((bf16[1424,128]{1,0:T(8,128)(2,1)S(1)}, bf16[1424,128]{1,0:T(8,128)(2,1)S(1)}, u32[]{:S(2)}, u32[]{:S(2)}) %collective-permute-start.6) | collective-permute-done | bytes 364576 | tf_op jit(solution)/shard_map/ppermute | solution.py:50
  49.0 1.7 %collective-permute-start.7 = (bf16[5696,128]{1,0:T(8,128)(2,1)S(1)}, bf16[5696,128]{1,0:T(8,128)(2,1)S(1)}, u32[]{:S(2)}, u32[]{:S(2)}) collective-permute-start(bf16[5696,128]{1,0:T(8,128)(2,1)S(1)} %pad_maximum_fusion.1), channel_id=1, source_target_pairs={{1,0},{0,1},{3,2},{2,3},{5,4},{4,5},{7,6},{6,7},{9,8},{8,9},{11,10... | collective-permute-start | bytes 4374536 | tf_op jit(solution)/shard_map/ppermute | solution.py:50
  50.7 2.9 %collective-permute-done.7.refs_8_ = bf16[5696,128]{1,0:T(8,128)(2,1)S(1)} collective-permute-done((bf16[5696,128]{1,0:T(8,128)(2,1)S(1)}, bf16[5696,128]{1,0:T(8,128)(2,1)S(1)}, u32[]{:S(2)}, u32[]{:S(2)}) %collective-permute-start.7) | collective-permute-done | bytes 1458208 | tf_op jit(solution)/shard_map/ppermute | solution.py:50
  53.6 1.3 shard_map.112
  54.9 1.8 %collective-permute-start.8 = (f32[208,640]{1,0:T(8,128)S(1)}, f32[208,640]{1,0:T(8,128)S(1)}, u32[]{:S(2)}, u32[]{:S(2)}) collective-permute-start(f32[208,640]{1,0:T(8,128)S(1)} %shard_map.112), channel_id=1, source_target_pairs={{16,0},{0,16},{17,1},{1,17},{18,2},{2,18},{19,3},{3,19},{20,4},{4,... | collective-permute-start | bytes 1597448 | tf_op jit(solution)/shard_map/ppermute | solution.py:46
  56.7 1.3 shard_map.113.refs_0_
  58.0 1.3 shard_map.114
  59.3 1.3 shard_map.115.refs_0_
  60.5 7.8 %collective-permute-done.8.refs_1_ = f32[208,640]{1,0:T(8,128)S(1)} collective-permute-done((f32[208,640]{1,0:T(8,128)S(1)}, f32[208,640]{1,0:T(8,128)S(1)}, u32[]{:S(2)}, u32[]{:S(2)}) %collective-permute-start.8) | collective-permute-done | bytes 532512 | tf_op jit(solution)/shard_map/ppermute | solution.py:46
  68.3 1.1 collective-permute-start.9
  69.5 1.4 %shard_map.116 = (f32[384,640]{1,0:T(8,128)}, f32[384,640]{1,0:T(8,128)}, f32[384,640]{1,0:T(8,128)}, bf16[208,640]{1,0:T(8,128)(2,1)S(1)}) custom-call(f32[208,640]{1,0:T(8,128)S(1)} %shard_map.113.refs_0_, f32[208,640]{1,0:T(8,128)S(1)} %collective-permute-done.8.refs_1_, f32[384,640]{1,0:T(8,128)S(1)} %bitcast.7, f32[384,640]{1,0:T(8,128)S(1)} %bitcast.9, ...), custom_call_target="tpu_custom_call" | custom-call | flops 133120 | bytes 133120 | tf_op jit(solution)/shard_map/pallas_call | solution.py:195
  70.9 1.7 %collective-permute-start.14 = (bf16[208,640]{1,0:T(8,128)(2,1)S(1)}, bf16[208,640]{1,0:T(8,128)(2,1)S(1)}, u32[]{:S(2)}, u32[]{:S(2)}) collective-permute-start(bf16[208,640]{1,0:T(8,128)(2,1)S(1)} %get-tuple-element.42.refs_0_), channel_id=1, source_target_pairs={{4,0},{5,1},{6,2},{7,3},{8,4},{9,5},{10,6},{11,7},{12,8},{13,9},{1... | collective-permute-start | bytes 798728 | tf_op jit(solution)/shard_map/ppermute | solution.py:46
  72.6 0.5 collective-permute-start.12
  73.1 1.5 %collective-permute-start.13 = (bf16[208,640]{1,0:T(8,128)(2,1)S(1)}, bf16[208,640]{1,0:T(8,128)(2,1)S(1)}, u32[]{:S(2)}, u32[]{:S(2)}) collective-permute-start(bf16[208,640]{1,0:T(8,128)(2,1)S(1)} %get-tuple-element.42.refs_0_), channel_id=1, source_target_pairs={{8,0},{9,1},{10,2},{11,3},{12,4},{13,5},{14,6},{15,7},{0,8},{1,9},... | collective-permute-start | bytes 798728 | tf_op jit(solution)/shard_map/ppermute | solution.py:46
  74.6 2.3 %collective-permute-start.10 = (bf16[208,640]{1,0:T(8,128)(2,1)S(1)}, bf16[208,640]{1,0:T(8,128)(2,1)S(1)}, u32[]{:S(2)}, u32[]{:S(2)}) collective-permute-start(bf16[208,640]{1,0:T(8,128)(2,1)S(1)} %get-tuple-element.42.refs_0_), channel_id=1, source_target_pairs={{12,0},{13,1},{14,2},{15,3},{0,4},{1,5},{2,6},{3,7},{4,8},{5,9},{6... | collective-permute-start | bytes 798728 | tf_op jit(solution)/shard_map/ppermute | solution.py:46
  76.9 1.8 %collective-permute-done.9.refs_1_ = f32[176,640]{1,0:T(8,128)S(1)} collective-permute-done((f32[176,640]{1,0:T(8,128)S(1)}, f32[176,640]{1,0:T(8,128)S(1)}, u32[]{:S(2)}, u32[]{:S(2)}) %collective-permute-start.9) | collective-permute-done | bytes 450592 | tf_op jit(solution)/shard_map/ppermute | solution.py:46
  78.7 1.3 %shard_map.117 = (f32[384,640]{1,0:T(8,128)}, f32[384,640]{1,0:T(8,128)}, f32[384,640]{1,0:T(8,128)}, bf16[176,640]{1,0:T(8,128)(2,1)S(1)}) custom-call(f32[176,640]{1,0:T(8,128)S(1)} %shard_map.115.refs_0_, f32[176,640]{1,0:T(8,128)S(1)} %collective-permute-done.9.refs_1_, ...), custom_call_target="tpu_custom_call", output_to_operand_aliasing={{0}: (5, {}), {1}: (6, {}), {2}: (7, {})} | custom-call | flops 112640 | bytes 112640 | tf_op jit(solution)/shard_map/pallas_call | solution.py:195
  80.1 0.2 collective-permute-start.11
  80.2 5.0 %collective-permute-done.11.refs_2_ = bf16[176,640]{1,0:T(8,128)(2,1)S(1)} collective-permute-done((bf16[176,640]{1,0:T(8,128)(2,1)S(1)}, bf16[176,640]{1,0:T(8,128)(2,1)S(1)}, u32[]{:S(2)}, u32[]{:S(2)}) %collective-permute-start.11) | collective-permute-done | bytes 225312 | tf_op jit(solution)/shard_map/ppermute | solution.py:50
  85.3 6.6 %collective-permute-done.13 = bf16[208,640]{1,0:T(8,128)(2,1)S(1)} collective-permute-done((bf16[208,640]{1,0:T(8,128)(2,1)S(1)}, bf16[208,640]{1,0:T(8,128)(2,1)S(1)}, u32[]{:S(2)}, u32[]{:S(2)}) %collective-permute-start.13) | collective-permute-done | bytes 266272 | tf_op jit(solution)/shard_map/ppermute | solution.py:46
  91.8 5.7 %collective-permute-done.10 = bf16[208,640]{1,0:T(8,128)(2,1)S(1)} collective-permute-done((bf16[208,640]{1,0:T(8,128)(2,1)S(1)}, bf16[208,640]{1,0:T(8,128)(2,1)S(1)}, u32[]{:S(2)}, u32[]{:S(2)}) %collective-permute-start.10) | collective-permute-done | bytes 266272 | tf_op jit(solution)/shard_map/ppermute | solution.py:46
  97.6 1.2 collective-permute-start.20
  98.9 0.8 collective-permute-start.15
  99.7 1.1 collective-permute-done.15.refs_1_
  100.8 0.4 collective-permute-done.16.refs_3_
  101.1 0.7 shard_map.118
  101.9 2.3 %collective-permute-start.17 = (bf16[176,640]{1,0:T(8,128)(2,1)S(1)}, bf16[176,640]{1,0:T(8,128)(2,1)S(1)}, u32[]{:S(2)}, u32[]{:S(2)}) collective-permute-start(bf16[176,640]{1,0:T(8,128)(2,1)S(1)} %get-tuple-element.55), channel_id=1, source_target_pairs={{12,0},{13,1},{14,2},{15,3},{0,4},{1,5},{2,6},{3,7},{4,8},{5,9},{6... | collective-permute-start | bytes 675848 | tf_op jit(solution)/shard_map/ppermute | solution.py:46
  104.1 1.3 collective-permute-start.19
  105.4 3.8 %collective-permute-done.17.refs_5_ = bf16[176,640]{1,0:T(8,128)(2,1)S(1)} collective-permute-done((bf16[176,640]{1,0:T(8,128)(2,1)S(1)}, bf16[176,640]{1,0:T(8,128)(2,1)S(1)}, u32[]{:S(2)}, u32[]{:S(2)}) %collective-permute-start.17) | collective-permute-done | bytes 225312 | tf_op jit(solution)/shard_map/ppermute | solution.py:46
  109.2 14.0 %collective-permute-done.18.refs_6_ = bf16[176,640]{1,0:T(8,128)(2,1)S(1)} collective-permute-done((bf16[176,640]{1,0:T(8,128)(2,1)S(1)}, bf16[176,640]{1,0:T(8,128)(2,1)S(1)}, u32[]{:S(2)}, u32[]{:S(2)}) %collective-permute-start.18) | collective-permute-done | bytes 225312 | tf_op jit(solution)/shard_map/ppermute | solution.py:46
  123.2 0.8 collective-permute-done.19.refs_7_
  123.9 0.6 shard_map.119
  124.6 0.6 collective-permute-start.21
  125.2 2.5 %shard_map.120.refs_1_ = bf16[384,2560]{1,0:T(8,128)(2,1)} custom-call(s32[16]{0:T(128)S(1)} %copy-done.5, bf16[208,640]{1,0:T(8,128)(2,1)S(1)} %get-tuple-element.42.refs_0_, bf16[208,640]{1,0:T(8,128)(2,1)S(1)} %collective-permute-done.12.refs_1_, bf16[624,640]{1,0:T(8,128)(2,1)S(1)} %constant_dynamic-update-slice_fusion.refs_2_, ...), custom_call_target="tpu_custom_call" | custom-call | flops 1 | bytes 16384 | tf_op jit(solution)/shard_map/pallas_call | solution.py:279
  127.6 0.6 shard_map.121
  (25 shorter events, 0.4 us)
Async XLA Ops:
  1.9 1.1 copy-start.3
  3.0 0.9 copy-start.4
  4.5 9.4 %collective-permute-start.1 = (bf16[1424,128]{1,0:T(8,128)(2,1)S(1)}, bf16[1424,128]{1,0:T(8,128)(2,1)S(1)}, u32[]{:S(2)}, u32[]{:S(2)}) collective-permute-start(bf16[1424,128]{1,0:T(8,128)(2,1)S(1)} %get-tuple-element.33), channel_id=1, source_target_pairs={{12,0},{13,1},{14,2},{15,3},{0,4},{1,5},{2,6},{3,7},{4,8},{5,9},{6... | collective-permute-start | bytes 1093640 | tf_op jit(solution)/shard_map/ppermute | solution.py:46
  5.9 17.8 %collective-permute-start.2 = (bf16[1424,128]{1,0:T(8,128)(2,1)S(1)}, bf16[1424,128]{1,0:T(8,128)(2,1)S(1)}, u32[]{:S(2)}, u32[]{:S(2)}) collective-permute-start(bf16[1424,128]{1,0:T(8,128)(2,1)S(1)} %get-tuple-element.34), channel_id=1, source_target_pairs={{4,0},{5,1},{6,2},{7,3},{8,4},{9,5},{10,6},{11,7},{12,8},{13,9},{1... | collective-permute-start | bytes 1093640 | tf_op jit(solution)/shard_map/ppermute | solution.py:46
  6.1 35.1 %collective-permute-start = (bf16[1424,128]{1,0:T(8,128)(2,1)S(1)}, bf16[1424,128]{1,0:T(8,128)(2,1)S(1)}, u32[]{:S(2)}, u32[]{:S(2)}) collective-permute-start(bf16[1424,128]{1,0:T(8,128)(2,1)S(1)} %get-tuple-element.32.refs_0_), channel_id=1, source_target_pairs={{2,0},{3,1},{0,2},{1,3},{6,4},{7,5},{4,6},{5,7},{10,8},{11,9},{8,1... | collective-permute-start | bytes 1093640 | tf_op jit(solution)/shard_map/ppermute | solution.py:50
  23.7 15.9 %collective-permute-start.5 = (bf16[1424,128]{1,0:T(8,128)(2,1)S(1)}, bf16[1424,128]{1,0:T(8,128)(2,1)S(1)}, u32[]{:S(2)}, u32[]{:S(2)}) collective-permute-start(bf16[1424,128]{1,0:T(8,128)(2,1)S(1)} %get-tuple-element.36), channel_id=1, source_target_pairs={{8,0},{9,1},{10,2},{11,3},{12,4},{13,5},{14,6},{15,7},{0,8},{1,9},... | collective-permute-start | bytes 1093640 | tf_op jit(solution)/shard_map/ppermute | solution.py:46
  23.9 24.9 %collective-permute-start.4 = (bf16[2848,128]{1,0:T(8,128)(2,1)S(1)}, bf16[2848,128]{1,0:T(8,128)(2,1)S(1)}, u32[]{:S(2)}, u32[]{:S(2)}) collective-permute-start(bf16[2848,128]{1,0:T(8,128)(2,1)S(1)} %pad_maximum_fusion.2), channel_id=1, source_target_pairs={{2,0},{3,1},{0,2},{1,3},{6,4},{7,5},{4,6},{5,7},{10,8},{11,9},{8,1... | collective-permute-start | bytes 2187272 | tf_op jit(solution)/shard_map/ppermute | solution.py:50
  39.6 9.3 %collective-permute-start.6 = (bf16[1424,128]{1,0:T(8,128)(2,1)S(1)}, bf16[1424,128]{1,0:T(8,128)(2,1)S(1)}, u32[]{:S(2)}, u32[]{:S(2)}) collective-permute-start(bf16[1424,128]{1,0:T(8,128)(2,1)S(1)} %collective-permute-done.5.refs_6_), channel_id=1, source_target_pairs={{2,0},{3,1},{0,2},{1,3},{6,4},{7,5},{4,6},{5,7},{10,8},{11,9},{8,1... | collective-permute-start | bytes 1093640 | tf_op jit(solution)/shard_map/ppermute | solution.py:50
  41.2 12.4 %copy-start.5 = (s32[16]{0:T(128)S(1)}, s32[16]{0:T(128)}, u32[]{:S(2)}) copy-start(s32[16]{0:T(128)} %plan_ref.10) | copy-start | bytes 196
  41.2 9.5 %collective-permute-start.3 = (bf16[5696,128]{1,0:T(8,128)(2,1)S(1)}, bf16[5696,128]{1,0:T(8,128)(2,1)S(1)}, u32[]{:S(2)}, u32[]{:S(2)}) collective-permute-start(bf16[5696,128]{1,0:T(8,128)(2,1)S(1)} %pad_maximum_fusion), channel_id=1, source_target_pairs={{1,0},{0,1},{3,2},{2,3},{5,4},{4,5},{7,6},{6,7},{9,8},{8,9},{11,10... | collective-permute-start | bytes 4374536 | tf_op jit(solution)/shard_map/ppermute | solution.py:50
  49.0 4.6 %collective-permute-start.7 = (bf16[5696,128]{1,0:T(8,128)(2,1)S(1)}, bf16[5696,128]{1,0:T(8,128)(2,1)S(1)}, u32[]{:S(2)}, u32[]{:S(2)}) collective-permute-start(bf16[5696,128]{1,0:T(8,128)(2,1)S(1)} %pad_maximum_fusion.1), channel_id=1, source_target_pairs={{1,0},{0,1},{3,2},{2,3},{5,4},{4,5},{7,6},{6,7},{9,8},{8,9},{11,10... | collective-permute-start | bytes 4374536 | tf_op jit(solution)/shard_map/ppermute | solution.py:50
  54.9 13.4 %collective-permute-start.8 = (f32[208,640]{1,0:T(8,128)S(1)}, f32[208,640]{1,0:T(8,128)S(1)}, u32[]{:S(2)}, u32[]{:S(2)}) collective-permute-start(f32[208,640]{1,0:T(8,128)S(1)} %shard_map.112), channel_id=1, source_target_pairs={{16,0},{0,16},{17,1},{1,17},{18,2},{2,18},{19,3},{3,19},{20,4},{4,... | collective-permute-start | bytes 1597448 | tf_op jit(solution)/shard_map/ppermute | solution.py:46
  59.2 10.2 %copy-start = (f32[1,384,640]{2,1,0:T(8,128)S(1)}, f32[1,384,640]{2,1,0:T(8,128)}, u32[]{:S(2)}) copy-start(f32[1,384,640]{2,1,0:T(8,128)} %param.13) | copy-start | bytes 2949124
  59.2 10.2 %copy-start.1 = (f32[1,384,640]{2,1,0:T(8,128)S(1)}, f32[1,384,640]{2,1,0:T(8,128)}, u32[]{:S(2)}) copy-start(f32[1,384,640]{2,1,0:T(8,128)} %param.14) | copy-start | bytes 2949124
  59.3 10.2 %copy-start.2 = (f32[1,384,640]{2,1,0:T(8,128)S(1)}, f32[1,384,640]{2,1,0:T(8,128)}, u32[]{:S(2)}) copy-start(f32[1,384,640]{2,1,0:T(8,128)} %param.15) | copy-start | bytes 2949124
  68.3 10.4 %collective-permute-start.9 = (f32[176,640]{1,0:T(8,128)S(1)}, f32[176,640]{1,0:T(8,128)S(1)}, u32[]{:S(2)}, u32[]{:S(2)}) collective-permute-start(f32[176,640]{1,0:T(8,128)S(1)} %shard_map.114), channel_id=1, source_target_pairs={{16,0},{0,16},{17,1},{1,17},{18,2},{2,18},{19,3},{3,19},{20,4},{4,... | collective-permute-start | bytes 1351688 | tf_op jit(solution)/shard_map/ppermute | solution.py:46
  70.9 9.3 %collective-permute-start.14 = (bf16[208,640]{1,0:T(8,128)(2,1)S(1)}, bf16[208,640]{1,0:T(8,128)(2,1)S(1)}, u32[]{:S(2)}, u32[]{:S(2)}) collective-permute-start(bf16[208,640]{1,0:T(8,128)(2,1)S(1)} %get-tuple-element.42.refs_0_), channel_id=1, source_target_pairs={{4,0},{5,1},{6,2},{7,3},{8,4},{9,5},{10,6},{11,7},{12,8},{13,9},{1... | collective-permute-start | bytes 798728 | tf_op jit(solution)/shard_map/ppermute | solution.py:46
  72.6 7.6 %collective-permute-start.12 = (bf16[208,640]{1,0:T(8,128)(2,1)S(1)}, bf16[208,640]{1,0:T(8,128)(2,1)S(1)}, u32[]{:S(2)}, u32[]{:S(2)}) collective-permute-start(bf16[208,640]{1,0:T(8,128)(2,1)S(1)} %get-tuple-element.42.refs_0_), channel_id=1, source_target_pairs={{2,0},{3,1},{0,2},{1,3},{6,4},{7,5},{4,6},{5,7},{10,8},{11,9},{8,1... | collective-permute-start | bytes 798728 | tf_op jit(solution)/shard_map/ppermute | solution.py:50
  73.1 18.7 %collective-permute-start.13 = (bf16[208,640]{1,0:T(8,128)(2,1)S(1)}, bf16[208,640]{1,0:T(8,128)(2,1)S(1)}, u32[]{:S(2)}, u32[]{:S(2)}) collective-permute-start(bf16[208,640]{1,0:T(8,128)(2,1)S(1)} %get-tuple-element.42.refs_0_), channel_id=1, source_target_pairs={{8,0},{9,1},{10,2},{11,3},{12,4},{13,5},{14,6},{15,7},{0,8},{1,9},... | collective-permute-start | bytes 798728 | tf_op jit(solution)/shard_map/ppermute | solution.py:46
  74.6 22.9 %collective-permute-start.10 = (bf16[208,640]{1,0:T(8,128)(2,1)S(1)}, bf16[208,640]{1,0:T(8,128)(2,1)S(1)}, u32[]{:S(2)}, u32[]{:S(2)}) collective-permute-start(bf16[208,640]{1,0:T(8,128)(2,1)S(1)} %get-tuple-element.42.refs_0_), channel_id=1, source_target_pairs={{12,0},{13,1},{14,2},{15,3},{0,4},{1,5},{2,6},{3,7},{4,8},{5,9},{6... | collective-permute-start | bytes 798728 | tf_op jit(solution)/shard_map/ppermute | solution.py:46
  80.1 5.2 %collective-permute-start.11 = (bf16[176,640]{1,0:T(8,128)(2,1)S(1)}, bf16[176,640]{1,0:T(8,128)(2,1)S(1)}, u32[]{:S(2)}, u32[]{:S(2)}) collective-permute-start(bf16[176,640]{1,0:T(8,128)(2,1)S(1)} %get-tuple-element.50.refs_0_), channel_id=1, source_target_pairs={{2,0},{3,1},{0,2},{1,3},{6,4},{7,5},{4,6},{5,7},{10,8},{11,9},{8,1... | collective-permute-start | bytes 675848 | tf_op jit(solution)/shard_map/ppermute | solution.py:50
  97.6 26.3 %collective-permute-start.20 = (bf16[624,640]{1,0:T(8,128)(2,1)S(1)}, bf16[624,640]{1,0:T(8,128)(2,1)S(1)}, u32[]{:S(2)}, u32[]{:S(2)}) collective-permute-start(bf16[624,640]{1,0:T(8,128)(2,1)S(1)} %constant_dynamic-update-slice_fusion.refs_2_), channel_id=1, source_target_pairs={{2,0},{3,1},{0,2},{1,3},{6,4},{7,5},{4,6},{5,7},{10,8},{11,9},{8,1... | collective-permute-start | bytes 2396168 | tf_op jit(solution)/shard_map/ppermute | solution.py:50
  98.9 1.9 %collective-permute-start.15 = (bf16[176,640]{1,0:T(8,128)(2,1)S(1)}, bf16[176,640]{1,0:T(8,128)(2,1)S(1)}, u32[]{:S(2)}, u32[]{:S(2)}) collective-permute-start(bf16[176,640]{1,0:T(8,128)(2,1)S(1)} %get-tuple-element.50.refs_0_), channel_id=1, source_target_pairs={{1,0},{0,1},{3,2},{2,3},{5,4},{4,5},{7,6},{6,7},{9,8},{8,9},{11,10... | collective-permute-start | bytes 675848 | tf_op jit(solution)/shard_map/ppermute | solution.py:50
  99.7 1.5 %collective-permute-start.16 = (bf16[176,640]{1,0:T(8,128)(2,1)S(1)}, bf16[176,640]{1,0:T(8,128)(2,1)S(1)}, u32[]{:S(2)}, u32[]{:S(2)}) collective-permute-start(bf16[176,640]{1,0:T(8,128)(2,1)S(1)} %collective-permute-done.11.refs_2_), channel_id=1, source_target_pairs={{1,0},{0,1},{3,2},{2,3},{5,4},{4,5},{7,6},{6,7},{9,8},{8,9},{11,10... | collective-permute-start | bytes 675848 | tf_op jit(solution)/shard_map/ppermute | solution.py:50
  101.9 7.4 %collective-permute-start.17 = (bf16[176,640]{1,0:T(8,128)(2,1)S(1)}, bf16[176,640]{1,0:T(8,128)(2,1)S(1)}, u32[]{:S(2)}, u32[]{:S(2)}) collective-permute-start(bf16[176,640]{1,0:T(8,128)(2,1)S(1)} %get-tuple-element.55), channel_id=1, source_target_pairs={{12,0},{13,1},{14,2},{15,3},{0,4},{1,5},{2,6},{3,7},{4,8},{5,9},{6... | collective-permute-start | bytes 675848 | tf_op jit(solution)/shard_map/ppermute | solution.py:46
  104.1 19.1 %collective-permute-start.18 = (bf16[176,640]{1,0:T(8,128)(2,1)S(1)}, bf16[176,640]{1,0:T(8,128)(2,1)S(1)}, u32[]{:S(2)}, u32[]{:S(2)}) collective-permute-start(bf16[176,640]{1,0:T(8,128)(2,1)S(1)} %get-tuple-element.56), channel_id=1, source_target_pairs={{8,0},{9,1},{10,2},{11,3},{12,4},{13,5},{14,6},{15,7},{0,8},{1,9},... | collective-permute-start | bytes 675848 | tf_op jit(solution)/shard_map/ppermute | solution.py:46
  104.1 19.8 %collective-permute-start.19 = (bf16[176,640]{1,0:T(8,128)(2,1)S(1)}, bf16[176,640]{1,0:T(8,128)(2,1)S(1)}, u32[]{:S(2)}, u32[]{:S(2)}) collective-permute-start(bf16[176,640]{1,0:T(8,128)(2,1)S(1)} %get-tuple-element.57), channel_id=1, source_target_pairs={{4,0},{5,1},{6,2},{7,3},{8,4},{9,5},{10,6},{11,7},{12,8},{13,9},{1... | collective-permute-start | bytes 675848 | tf_op jit(solution)/shard_map/ppermute | solution.py:46
  124.6 3.0 %collective-permute-start.21 = (bf16[4,208,640]{2,1,0:T(8,128)(2,1)S(1)}, bf16[4,208,640]{2,1,0:T(8,128)(2,1)S(1)}, u32[]{:S(2)}, u32[]{:S(2)}) collective-permute-start(bf16[4,208,640]{2,1,0:T(8,128)(2,1)S(1)} %shard_map.119), channel_id=1, source_target_pairs={{1,0},{0,1},{3,2},{2,3},{5,4},{4,5},{7,6},{6,7},{9,8},{8,9},{11,10... | collective-permute-start | bytes 3194888 | tf_op jit(solution)/shard_map/ppermute | solution.py:50
where the time goes:
time: 130 us; the launch traced here: 128 us
  waiting for transfers between devices  87.4 us (67%)
  starting transfers between devices  23.6 us (18%)
  Pallas kernels  12.8 us (10%)
  local copies, waits for them, and re-layouts  2.12 us (2%)
  between operations  2.11 us (2%)
    ppermute x11, waiting for transfers between devices, from_behind(): return lax.ppermute(block, axis, route)  71.2 us
    ppermute x11, waiting for transfers between devices, from_mate(): lax.ppermute(block, axis, [(i ^ bit, i) for i in range(lax.axis_size(axis...  16.2 us
    ppermute x11, starting transfers between devices, from_behind(): return lax.ppermute(block, axis, route)  13.7 us
    ppermute x11, starting transfers between devices, from_mate(): lax.ppermute(block, axis, [(i ^ bit, i) for i in range(lax.axis_size(axis...  9.86 us
    pallas_call x6, Pallas kernels, call(): pl.pallas_call(kernel, out_shape=tuple(out_shapes), in_specs=[SMEM] * len...  6.43 us
    pallas_call x2, Pallas kernels, assemble(): pl.pallas_call(functools.partial(assemble_kernel, owner_count, span, late...  3.08 us
    pallas_call x2, Pallas kernels, update(): pl.pallas_call(functools.partial(update_kernel, len(terms), len(held), sp...  2.72 us
  transfers between devices with their start and end apart: 22, of which 15 were waited for; matrix products, arithmetic and copies ran while one was open for 0% of the time, Pallas kernels for 8%

commit v1 on v0

--- a/solution.py
+++ b/solution.py
@@ -82,18 +82,11 @@
     return own // owner_count, own % owner_count
 
 
-def message_kernel(owner_count, slot_ref, live_ref, hidden_hbm, grad_hbm, *refs):
-    *message_refs, hidden_ref, grad_ref, sems = refs
-    loads = [
-        pltpu.make_async_copy(hidden_hbm, hidden_ref, sems.at[0]),
-        pltpu.make_async_copy(grad_hbm, grad_ref, sems.at[1]),
-    ]
-    for load in loads:
-        load.start()
-    for load in loads:
-        load.wait()
+def message_kernel(owner_count, spans, slot_ref, live_ref, hidden_ref, grad_ref, *message_refs):
     own_block, _ = place(owner_count)
+    groups = lax.axis_size("dp")
     hidden_units, tok_rows = hidden_ref.shape
+    share_rows = hidden_units // groups
     block_width = grad_ref.shape[1] // QUART
     parts = block_width // LANES
     live = live_ref[0]
@@ -101,7 +94,14 @@
     kept = lax.broadcasted_iota(jnp.int32, (tok_rows, LANES), 0) < live
     meta = jnp.full((META_ROWS, LANES), slot.astype(jnp.float32)).astype(jnp.bfloat16)
 
-    for step, message in enumerate(message_refs):
+    def put_hidden(message, row, span):
+        first, length = span
+        for group in range(groups):
+            start = group * share_rows + first
+            message[row : row + length, :] = hidden_ref[start : start + length, :]
+            row += length
+
+    for step, message in enumerate(message_refs[:QUART]):
         target = lax.rem(own_block + step, QUART)
         for part in range(parts):
             start = pl.multiple_of(target * block_width + part * LANES, LANES)
@@ -110,10 +110,12 @@
             message[row : row + tok_rows, :] = jnp.where(kept, columns, 0.0).astype(jnp.bfloat16)
         row = parts * tok_rows
         message[row : row + META_ROWS, :] = meta
-        message[row + META_ROWS :, :] = hidden_ref[...]
-
-
-def partial_kernel(owner_count, tok_rows, share_rows, where, base, steps, plan_ref, *refs):
+        put_hidden(message, row + META_ROWS, spans[0])
+    for message, span in zip(message_refs[QUART:], spans[1:]):
+        put_hidden(message, 0, span)
+
+
+def partial_kernel(owner_count, tok_rows, where, base, steps, plan_ref, *refs):
     totals = refs[-len(steps) :]
     own_block, own_expert = place(owner_count)
     group, groups = lax.axis_index("dp"), lax.axis_size("dp")
@@ -123,13 +125,13 @@
     bits = []
     for first in range(0, len(where), 16):
         packed = jnp.zeros((META_ROWS, LANES), jnp.float32)
-        for at, (_, (ref, row)) in enumerate(where[first : first + 16]):
-            meta = refs[ref][row + parts * tok_rows : row + parts * tok_rows + META_ROWS, :]
+        for at, (_, (head, row), _) in enumerate(where[first : first + 16]):
+            meta = refs[head][row + parts * tok_rows : row + parts * tok_rows + META_ROWS, :]
             packed = packed + meta.astype(jnp.float32) * float(1 << at)
         bits.append(jnp.max(packed).astype(jnp.int32))
     for total in totals:
         total[...] = jnp.zeros_like(total)
-    for at, ((step, mate), (ref, row)) in enumerate(where):
+    for at, ((step, mate), (head, head_row), (tail, tail_row)) in enumerate(where):
         source_expert = own_expert ^ mate
         source = lax.rem(own_block + QUART - step, QUART) * owner_count + source_expert
         is_replica = ((bits[at // 16] >> (at % 16)) & 1) == 1
@@ -138,16 +140,19 @@
         @pl.when(target == own_expert)
         def _():
             columns = jnp.concatenate(
-                [refs[ref][row + p * tok_rows : row + (p + 1) * tok_rows, :] for p in range(parts)],
+                [
+                    refs[head][head_row + p * tok_rows : head_row + (p + 1) * tok_rows, :]
+                    for p in range(parts)
+                ],
                 axis=1,
             )
             for total, ahead in zip(totals, steps):
-                start = row + base + lax.rem(group + ahead, groups) * share_rows
+                start = tail_row + base + lax.rem(group + ahead, groups) * rows
 
                 @pl.loop(0, rows // chunk)
                 def _(i):
                     term = jnp.dot(
-                        refs[ref][pl.ds(pl.multiple_of(start + i * chunk, 16), chunk), :],
+                        refs[tail][pl.ds(pl.multiple_of(start + i * chunk, 16), chunk), :],
                         columns,
                         preferred_element_type=jnp.float32,
                     )
@@ -225,15 +230,13 @@
     held, out = refs[:-1], refs[-1]
     own_block, own_expert = place(owner_count)
     wanted = plan_ref[own_block * owner_count + (own_expert ^ 1)]
-    half = owner_count // 2
-    rows = held[0].shape[0]
-    for pair in range(half):
+    rows = out.shape[1]
+    for pair, blocks in enumerate(held):
 
         @pl.when((wanted ^ own_expert) >> 1 == pair)
         def _():
-            out[0] = held[pair][...]
-            for step in range(1, QUART):
-                out[step] = held[half + pair][(step - 1) * rows : step * rows, :]
+            for step in range(QUART):
+                out[step] = blocks[step * rows : (step + 1) * rows, :]
 
 
 def assemble_kernel(owner_count, span, later, plan_ref, *refs):
@@ -263,14 +266,13 @@
 
         return
 
-    near, far, received = blocks[:half], blocks[half : 2 * half], blocks[2 * half :]
+    held, received = blocks[:half], blocks[half:]
     put(received, first + rows)
     for pair in range(half):
 
         @pl.when(apart == 2 * pair)
         def _():
-            sources = [far[pair].at[pl.ds(step * rows, rows), :] for step in range(QUART - 1)]
-            put([near[pair], *sources], first)
+            put([held[pair].at[pl.ds(step * rows, rows), :] for step in range(QUART)], first)
 
 
 def assemble(owner_count, span, plan, blocks, shape, held=None):
@@ -302,22 +304,14 @@
     spans = ((0, lead), (lead, share_rows - lead))
 
     head_rows = (block_width // LANES) * tok_rows + META_ROWS
-    outs = [shape((head_rows + hidden_units, LANES), jnp.bfloat16)] * QUART
-    messages = pl.pallas_call(
-        functools.partial(message_kernel, owner_count),
-        out_shape=tuple(outs),
-        in_specs=[SMEM, SMEM, ANYWHERE, ANYWHERE],
-        out_specs=tuple([VMEM] * len(outs)),
-        scratch_shapes=[
-            pltpu.VMEM(hidden_rows.shape, hidden_rows.dtype),
-            pltpu.VMEM(grad_rows.shape, grad_rows.dtype),
-            pltpu.SemaphoreType.DMA((2,)),
-        ],
-        compiler_params=pltpu.CompilerParams(
-            vmem_limit_bytes=vmem_for(hidden_rows, grad_rows, *outs)
-        ),
-        cost_estimate=pl.CostEstimate(flops=1, bytes_accessed=1 << 14, transcendentals=0),
-    )(block_slot, live_rows, hidden_rows, grad_rows)
+    outs = [shape((head_rows + groups * lead, LANES), jnp.bfloat16)] * QUART
+    outs += [shape((groups * (share_rows - lead), LANES), jnp.bfloat16)]
+    messages = call(
+        functools.partial(message_kernel, owner_count, spans),
+        outs,
+        (block_slot, live_rows),
+        (hidden_rows, grad_rows),
+    )
 
     def across(block, step):
         return from_behind(block, "expert", step * owner_count) if step else block
@@ -326,35 +320,37 @@
     other_bits = [1 << i for i in reversed(range(first_bit.bit_length() - 1))]
     own = [([(0, 0)], messages[0])]
     sides = [([(step, 0)], across(messages[step], step)) for step in (1, 3)]
-    own += [exchange(own, first_bit)]
-    last = across(after(messages[2], *(block for _, block in sides)), 2)
+    keys, block = exchange(own, first_bit)
+    own += [(keys, after(block, *(side for _, side in sides))), *sides]
+    last = [([(2, 0)], across(after(messages[2], own[1][1]), 2))]
     crossed = [exchange(sides, first_bit)]
-    own += sides
+    last_crossed = exchange(last, first_bit)
     for bit in other_bits:
         own += [exchange(own, bit)]
-    last = [([(2, 0)], last)]
-    last += [exchange(last, first_bit)]
-    last = crossed + last
+        last += [exchange(last, bit)]
+    later = after(messages[QUART], last[-1][1], crossed[0][1])
+    rest = [([(0, 0)], messages[QUART])]
+    rest += [([(step, 0)], across(later, step)) for step in (1, 2, 3)]
+    keys, block = last_crossed
+    crossed += [(keys, after(block, *(part for _, part in rest[1:])))]
     for bit in other_bits:
-        last += [exchange(last, bit)]
+        crossed += [exchange(crossed, bit)]
+    last += crossed
     heads = own + last
     head_at = places(heads, 0)
+    rests, rest_at = [], {}
 
     def partials(at, steps, wait_for):
-        first, rows = spans[at]
+        rows = spans[at][1]
+        packs = heads + rests if at else heads
+        where = [(key, found, rest_at[key] if at else found) for key, found in head_at.items()]
         return call(
             functools.partial(
-                partial_kernel,
-                owner_count,
-                tok_rows,
-                share_rows,
-                tuple(head_at.items()),
-                head_rows + first,
-                steps,
+                partial_kernel, owner_count, tok_rows, where, 0 if at else head_rows, steps
             ),
             [shape((rows, block_width), jnp.float32)] * len(steps),
             (after(replica_plan, *wait_for),),
-            [block for _, block in heads],
+            [block for _, block in packs],
             2 * len(steps) * rows * tok_rows * block_width * QUART,
         )
 
@@ -365,6 +361,18 @@
     far_one = partials(0, ahead, ())
     came_one = [from_behind(p, "dp", step) for step, p in zip(ahead, far_one)]
     near_one = partials(0, (0,), far_one)
+
+    keys, parts = zip(*rest)
+    stack = jnp.concatenate(parts)
+    rest = [(sum(keys, []), stack)]
+    rest += [exchange(rest, first_bit)]
+    for pack in rest:
+        group = [pack]
+        for bit in other_bits:
+            group += [exchange(group, bit)]
+        rests += group
+    rest_at.update(places(rests, len(heads)))
+
     far_two = partials(1, ahead, near_one)
     near_two = partials(1, (0,), far_two)
     came_one = [after(term, *near_two) for term in came_one]
@@ -379,9 +387,7 @@
     *held, fresh_two = update((*near_two, *came_two), states, spans[1], held)
 
     mates_two = gather_mates(fresh_two, "expert", owner_count)
-    near_wide = gather_mates(fresh_one, "expert", owner_count, 2)[::2]
-    crossed = mates_two[owner_count // 2], near_wide[-1]
-    lines[1:] = [after(line, *crossed) for line in lines[1:]]
+    lines[1:] = [after(line, mates_two[owner_count // 2]) for line in lines[1:]]
     chosen = call(
         functools.partial(choose_kernel, owner_count),
         [block(spans[1][1])] * QUART,
@@ -390,19 +396,18 @@
     )
     received = [across(c, step) for step, c in enumerate(chosen)]
 
-    stacked = jnp.concatenate(lines[1:])
-    far_wide = gather_mates(stacked, "expert", owner_count, 2)[::2]
+    wide = gather_mates(jnp.concatenate(lines), "expert", owner_count, 2)[::2]
     (offer,) = call(
         functools.partial(offer_kernel, owner_count),
         [shape((QUART, spans[0][1], block_width), jnp.bfloat16)],
-        (after(replica_plan, *received[1:]),),
-        (*near_wide, *far_wide),
+        (replica_plan,),
+        wide,
     )
     result = shape((share_rows, QUART * block_width), jnp.bfloat16)
     placed = assemble(
-        owner_count, spans[0], replica_plan, [*near_wide, *far_wide, *received], result
+        owner_count, spans[0], replica_plan, [*wide, *received], result
     )
-    offer = from_mate(offer, "expert", 1)
+    offer = from_mate(after(offer, *received[1:]), "expert", 1)
     replica_weight = assemble(owner_count, spans[0], replica_plan, [offer], result, placed)
     return (*(state[None] for state in held), replica_weight[None])
 

time: 130 us -> 125 us (0.962)
  waiting for transfers between devices: 87.4 us -> 71.3 us
  starting transfers between devices: 23.6 us -> 35.1 us
    ppermute x11 -> x14, waiting for transfers between devices: 71.2 us -> 40.9 us  [from_behind(): return lax.ppermute(block, axis, route)]
    ppermute x11 -> x14, waiting for transfers between devices: 16.2 us -> 30.4 us  [from_mate(): lax.ppermute(block, axis, [(i ^ bit, i) for i in range(lax.axis_size(axis...]
    ppermute x11 -> x14, starting transfers between devices: 9.86 us -> 20.1 us  [from_mate(): lax.ppermute(block, axis, [(i ^ bit, i) for i in range(lax.axis_size(axis...]
    ppermute x11 -> x14, starting transfers between devices: 13.7 us -> 15 us  [from_behind(): return lax.ppermute(block, axis, route)]
    pallas_call x6 -> x7, Pallas kernels: 6.43 us -> 7.47 us  [call(): pl.pallas_call(kernel, out_shape=tuple(out_shapes), in_specs=[SMEM] * len...]
  transfers between devices with their start and end apart: 22 -> 28, of which waited for: 15 -> 16; matrix products, arithmetic and copies ran while one was open for 0% -> 0% of each run, Pallas kernels for 8% -> 10%
where the time goes in v1:
time: 125 us; the launch traced here: 124 us
  waiting for transfers between devices  71.3 us (57%)
  starting transfers between devices  35.1 us (28%)
  Pallas kernels  13.3 us (11%)
  local copies, waits for them, and re-layouts  2.21 us (2%)
  between operations  2.18 us (2%)
    ppermute x14, waiting for transfers between devices, from_behind(): return lax.ppermute(block, axis, route)  40.9 us
    ppermute x14, waiting for transfers between devices, from_mate(): lax.ppermute(block, axis, [(i ^ bit, i) for i in range(lax.axis_size(axis...  30.4 us
    ppermute x14, starting transfers between devices, from_mate(): lax.ppermute(block, axis, [(i ^ bit, i) for i in range(lax.axis_size(axis...  20.1 us
    ppermute x14, starting transfers between devices, from_behind(): return lax.ppermute(block, axis, route)  15 us
    pallas_call x7, Pallas kernels, call(): pl.pallas_call(kernel, out_shape=tuple(out_shapes), in_specs=[SMEM] * len...  7.47 us
    pallas_call x2, Pallas kernels, assemble(): pl.pallas_call(functools.partial(assemble_kernel, owner_count, span, late...  3.08 us
    pallas_call x2, Pallas kernels, update(): pl.pallas_call(functools.partial(update_kernel, len(terms), len(held), sp...  2.7 us
  transfers between devices with their start and end apart: 28, of which 16 were waited for; matrix products, arithmetic and copies ran while one was open for 0% of the time, Pallas kernels for 10%

profile of v1, /device:TPU:9, one launch (start us, length us, event | category | flops | bytes accessed | tf_op | source)
XLA Modules:
  0.0 124.2 jit_solution(17359290068009889827)
XLA Ops:
  1.9 1.1 copy-done.3
  3.0 0.9 copy-done.4
  4.1 1.3 %collective-permute-start.1 = (bf16[1072,128]{1,0:T(8,128)(2,1)S(1)}, bf16[1072,128]{1,0:T(8,128)(2,1)S(1)}, u32[]{:S(2)}, u32[]{:S(2)}) collective-permute-start(bf16[1072,128]{1,0:T(8,128)(2,1)S(1)} %get-tuple-element.37), channel_id=1, source_target_pairs={{12,0},{13,1},{14,2},{15,3},{0,4},{1,5},{2,6},{3,7},{4,8},{5,9},{6... | collective-permute-start | bytes 823304 | tf_op jit(solution)/shard_map/ppermute | solution.py:46
  5.6 1.2 collective-permute-start
  6.8 4.8 %collective-permute-done.1.refs_2_ = bf16[1072,128]{1,0:T(8,128)(2,1)S(1)} collective-permute-done((bf16[1072,128]{1,0:T(8,128)(2,1)S(1)}, bf16[1072,128]{1,0:T(8,128)(2,1)S(1)}, u32[]{:S(2)}, u32[]{:S(2)}) %collective-permute-start.1) | collective-permute-done | bytes 274464 | tf_op jit(solution)/shard_map/ppermute | solution.py:46
  11.6 7.8 %collective-permute-done.2.refs_3_ = bf16[1072,128]{1,0:T(8,128)(2,1)S(1)} collective-permute-done((bf16[1072,128]{1,0:T(8,128)(2,1)S(1)}, bf16[1072,128]{1,0:T(8,128)(2,1)S(1)}, u32[]{:S(2)}, u32[]{:S(2)}) %collective-permute-start.2) | collective-permute-done | bytes 274464 | tf_op jit(solution)/shard_map/ppermute | solution.py:46
  19.6 1.3 %collective-permute-start.6 = (bf16[2144,128]{1,0:T(8,128)(2,1)S(1)}, bf16[2144,128]{1,0:T(8,128)(2,1)S(1)}, u32[]{:S(2)}, u32[]{:S(2)}) collective-permute-start(bf16[2144,128]{1,0:T(8,128)(2,1)S(1)} %pad_maximum_fusion.2), channel_id=1, source_target_pairs={{2,0},{3,1},{0,2},{1,3},{6,4},{7,5},{4,6},{5,7},{10,8},{11,9},{8,1... | collective-permute-start | bytes 1646600 | tf_op jit(solution)/shard_map/ppermute | solution.py:50
  20.9 10.5 %collective-permute-done.4.refs_5_ = bf16[1072,128]{1,0:T(8,128)(2,1)S(1)} collective-permute-done((bf16[1072,128]{1,0:T(8,128)(2,1)S(1)}, bf16[1072,128]{1,0:T(8,128)(2,1)S(1)}, u32[]{:S(2)}, u32[]{:S(2)}) %collective-permute-start.4) | collective-permute-done | bytes 274464 | tf_op jit(solution)/shard_map/ppermute | solution.py:46
  31.4 0.8 collective-permute-start.5
  32.3 1.2 collective-permute-start.7
  33.5 0.9 collective-permute-start.8
  34.4 4.0 %collective-permute-start.9 = (bf16[352,128]{1,0:T(8,128)(2,1)S(1)}, bf16[352,128]{1,0:T(8,128)(2,1)S(1)}, u32[]{:S(2)}, u32[]{:S(2)}) collective-permute-start(bf16[352,128]{1,0:T(8,128)(2,1)S(1)} %get-tuple-element.43), channel_id=1, source_target_pairs={{8,0},{9,1},{10,2},{11,3},{12,4},{13,5},{14,6},{15,7},{0,8},{1,9},... | collective-permute-start | bytes 270344 | tf_op jit(solution)/shard_map/ppermute | solution.py:46
  38.5 1.0 collective-permute-start.3
  39.5 1.0 collective-permute-done.7.refs_8_
  40.5 3.7 %collective-permute-done.9 = bf16[352,128]{1,0:T(8,128)(2,1)S(1)} collective-permute-done((bf16[352,128]{1,0:T(8,128)(2,1)S(1)}, bf16[352,128]{1,0:T(8,128)(2,1)S(1)}, u32[]{:S(2)}, u32[]{:S(2)}) %collective-permute-start.9) | collective-permute-done | bytes 90144 | tf_op jit(solution)/shard_map/ppermute | solution.py:46
  44.2 1.6 %collective-permute-done.10 = bf16[352,128]{1,0:T(8,128)(2,1)S(1)} collective-permute-done((bf16[352,128]{1,0:T(8,128)(2,1)S(1)}, bf16[352,128]{1,0:T(8,128)(2,1)S(1)}, u32[]{:S(2)}, u32[]{:S(2)}) %collective-permute-start.10) | collective-permute-done | bytes 90144 | tf_op jit(solution)/shard_map/ppermute | solution.py:46
  45.9 1.2 collective-permute-start.11
  47.2 1.2 collective-permute-start.13
  48.3 0.7 collective-permute-done.11.refs_9_
  49.1 1.5 %shard_map.112 = f32[208,640]{1,0:T(8,128)S(1)} custom-call(s32[16]{0:T(128)S(1)} %copy-done.5, bf16[1072,128]{1,0:T(8,128)(2,1)S(1)} %get-tuple-element.36.refs_0_, bf16[1072,128]{1,0:T(8,128)(2,1)S(1)} %collective-permute-done.refs_1_, bf16[1072,128]{1,0:T(8,128)(2,1)S(1)} %collective-permute-done.1.refs_2_, ...), custom_call_target="tpu_custom_call" | custom-call | flops 2129920 | bytes 76928 | tf_op jit(solution)/shard_map/pallas_call | solution.py:33
  50.6 0.8 collective-permute-start.15
  51.4 1.3 %collective-permute-start.12 = (bf16[1408,128]{1,0:T(8,128)(2,1)S(1)}, bf16[1408,128]{1,0:T(8,128)(2,1)S(1)}, u32[]{:S(2)}, u32[]{:S(2)}) collective-permute-start(bf16[1408,128]{1,0:T(8,128)(2,1)S(1)} %constant_dynamic-update-slice_fusion.refs_10_), channel_id=1, source_target_pairs={{1,0},{0,1},{3,2},{2,3},{5,4},{4,5},{7,6},{6,7},{9,8},{8,9},{11,10... | collective-permute-start | bytes 1081352 | tf_op jit(solution)/shard_map/ppermute | solution.py:50
  52.8 4.5 %collective-permute-done.13.refs_12_ = bf16[1408,128]{1,0:T(8,128)(2,1)S(1)} collective-permute-done((bf16[1408,128]{1,0:T(8,128)(2,1)S(1)}, bf16[1408,128]{1,0:T(8,128)(2,1)S(1)}, u32[]{:S(2)}, u32[]{:S(2)}) %collective-permute-start.13) | collective-permute-done | bytes 360480 | tf_op jit(solution)/shard_map/ppermute | solution.py:50
  57.2 0.8 collective-permute-start.14
  58.1 1.5 %shard_map.113.refs_0_ = f32[208,640]{1,0:T(8,128)S(1)} custom-call(s32[16]{0:T(128)S(1)} %copy-done.5, bf16[1072,128]{1,0:T(8,128)(2,1)S(1)} %get-tuple-element.36.refs_0_, bf16[1072,128]{1,0:T(8,128)(2,1)S(1)} %collective-permute-done.refs_1_, bf16[1072,128]{1,0:T(8,128)(2,1)S(1)} %collective-permute-done.1.refs_2_, ...), custom_call_target="tpu_custom_call" | custom-call | flops 2129920 | bytes 76928 | tf_op jit(solution)/shard_map/pallas_call | solution.py:33
  59.6 1.5 %shard_map.114 = f32[176,640]{1,0:T(8,128)S(1)} custom-call(s32[16]{0:T(128)S(1)} %copy-done.5, bf16[1072,128]{1,0:T(8,128)(2,1)S(1)} %get-tuple-element.36.refs_0_, bf16[1072,128]{1,0:T(8,128)(2,1)S(1)} %collective-permute-done.refs_1_, bf16[1072,128]{1,0:T(8,128)(2,1)S(1)} %collective-permute-done.1.refs_2_, ...), custom_call_target="tpu_custom_call" | custom-call | flops 1802240 | bytes 98176 | tf_op jit(solution)/shard_map/pallas_call | solution.py:33
  61.1 1.5 %shard_map.115.refs_0_ = f32[176,640]{1,0:T(8,128)S(1)} custom-call(s32[16]{0:T(128)S(1)} %copy-done.5, bf16[1072,128]{1,0:T(8,128)(2,1)S(1)} %get-tuple-element.36.refs_0_, bf16[1072,128]{1,0:T(8,128)(2,1)S(1)} %collective-permute-done.refs_1_, bf16[1072,128]{1,0:T(8,128)(2,1)S(1)} %collective-permute-done.1.refs_2_, ...), custom_call_target="tpu_custom_call" | custom-call | flops 1802240 | bytes 98176 | tf_op jit(solution)/shard_map/pallas_call | solution.py:33
  62.6 1.6 %collective-permute-done.15.refs_1_ = f32[208,640]{1,0:T(8,128)S(1)} collective-permute-done((f32[208,640]{1,0:T(8,128)S(1)}, f32[208,640]{1,0:T(8,128)S(1)}, u32[]{:S(2)}, u32[]{:S(2)}) %collective-permute-start.15) | collective-permute-done | bytes 532512 | tf_op jit(solution)/shard_map/ppermute | solution.py:46
  64.2 1.4 %shard_map.116 = (f32[384,640]{1,0:T(8,128)}, f32[384,640]{1,0:T(8,128)}, f32[384,640]{1,0:T(8,128)}, bf16[208,640]{1,0:T(8,128)(2,1)S(1)}) custom-call(f32[208,640]{1,0:T(8,128)S(1)} %shard_map.113.refs_0_, f32[208,640]{1,0:T(8,128)S(1)} %collective-permute-done.15.refs_1_, f32[384,640]{1,0:T(8,128)S(1)} %bitcast.7, f32[384,640]{1,0:T(8,128)S(1)} %bitcast.9, ...), custom_call_target="tpu_custom_call" | custom-call | flops 133120 | bytes 133120 | tf_op jit(solution)/shard_map/pallas_call | solution.py:200
  65.7 0.9 collective-permute-start.19
  66.6 2.3 %collective-permute-start.17 = (bf16[208,640]{1,0:T(8,128)(2,1)S(1)}, bf16[208,640]{1,0:T(8,128)(2,1)S(1)}, u32[]{:S(2)}, u32[]{:S(2)}) collective-permute-start(bf16[208,640]{1,0:T(8,128)(2,1)S(1)} %get-tuple-element.50), channel_id=1, source_target_pairs={{12,0},{13,1},{14,2},{15,3},{0,4},{1,5},{2,6},{3,7},{4,8},{5,9},{6... | collective-permute-start | bytes 798728 | tf_op jit(solution)/shard_map/ppermute | solution.py:46
  68.9 6.2 %collective-permute-done.16.refs_1_ = f32[176,640]{1,0:T(8,128)S(1)} collective-permute-done((f32[176,640]{1,0:T(8,128)S(1)}, f32[176,640]{1,0:T(8,128)S(1)}, u32[]{:S(2)}, u32[]{:S(2)}) %collective-permute-start.16) | collective-permute-done | bytes 450592 | tf_op jit(solution)/shard_map/ppermute | solution.py:46
  75.1 1.3 %shard_map.117 = (f32[384,640]{1,0:T(8,128)}, f32[384,640]{1,0:T(8,128)}, f32[384,640]{1,0:T(8,128)}, bf16[176,640]{1,0:T(8,128)(2,1)S(1)}) custom-call(f32[176,640]{1,0:T(8,128)S(1)} %shard_map.115.refs_0_, f32[176,640]{1,0:T(8,128)S(1)} %collective-permute-done.16.refs_1_, ...), custom_call_target="tpu_custom_call", output_to_operand_aliasing={{0}: (5, {}), {1}: (6, {}), {2}: (7, {})} | custom-call | flops 112640 | bytes 112640 | tf_op jit(solution)/shard_map/pallas_call | solution.py:200
  76.4 3.5 %collective-permute-start.18 = (bf16[176,640]{1,0:T(8,128)(2,1)S(1)}, bf16[176,640]{1,0:T(8,128)(2,1)S(1)}, u32[]{:S(2)}, u32[]{:S(2)}) collective-permute-start(bf16[176,640]{1,0:T(8,128)(2,1)S(1)} %get-tuple-element.58.refs_0_), channel_id=1, source_target_pairs={{2,0},{3,1},{0,2},{1,3},{6,4},{7,5},{4,6},{5,7},{10,8},{11,9},{8,1... | collective-permute-start | bytes 675848 | tf_op jit(solution)/shard_map/ppermute | solution.py:50
  79.9 5.7 %collective-permute-done.18.refs_2_ = bf16[176,640]{1,0:T(8,128)(2,1)S(1)} collective-permute-done((bf16[176,640]{1,0:T(8,128)(2,1)S(1)}, bf16[176,640]{1,0:T(8,128)(2,1)S(1)}, u32[]{:S(2)}, u32[]{:S(2)}) %collective-permute-start.18) | collective-permute-done | bytes 225312 | tf_op jit(solution)/shard_map/ppermute | solution.py:50
  85.6 3.4 %collective-permute-done.17 = bf16[208,640]{1,0:T(8,128)(2,1)S(1)} collective-permute-done((bf16[208,640]{1,0:T(8,128)(2,1)S(1)}, bf16[208,640]{1,0:T(8,128)(2,1)S(1)}, u32[]{:S(2)}, u32[]{:S(2)}) %collective-permute-start.17) | collective-permute-done | bytes 266272 | tf_op jit(solution)/shard_map/ppermute | solution.py:46
  89.1 5.0 %collective-permute-start.21 = (bf16[832,640]{1,0:T(8,128)(2,1)S(1)}, bf16[832,640]{1,0:T(8,128)(2,1)S(1)}, u32[]{:S(2)}, u32[]{:S(2)}) collective-permute-start(bf16[832,640]{1,0:T(8,128)(2,1)S(1)} %constant_dynamic-update-slice_fusion.4.refs_0_), channel_id=1, source_target_pairs={{2,0},{3,1},{0,2},{1,3},{6,4},{7,5},{4,6},{5,7},{10,8},{11,9},{8,1... | collective-permute-start | bytes 3194888 | tf_op jit(solution)/shard_map/ppermute | solution.py:50
  94.2 0.5 collective-permute-start.23
  94.7 1.0 collective-permute-done.22.refs_1_
  96.0 0.7 shard_map.119
  96.7 2.0 %collective-permute-start.24 = (bf16[176,640]{1,0:T(8,128)(2,1)S(1)}, bf16[176,640]{1,0:T(8,128)(2,1)S(1)}, u32[]{:S(2)}, u32[]{:S(2)}) collective-permute-start(bf16[176,640]{1,0:T(8,128)(2,1)S(1)} %get-tuple-element.63), channel_id=1, source_target_pairs={{12,0},{13,1},{14,2},{15,3},{0,4},{1,5},{2,6},{3,7},{4,8},{5,9},{6... | collective-permute-start | bytes 675848 | tf_op jit(solution)/shard_map/ppermute | solution.py:46
  98.6 2.2 %collective-permute-start.25 = (bf16[176,640]{1,0:T(8,128)(2,1)S(1)}, bf16[176,640]{1,0:T(8,128)(2,1)S(1)}, u32[]{:S(2)}, u32[]{:S(2)}) collective-permute-start(bf16[176,640]{1,0:T(8,128)(2,1)S(1)} %get-tuple-element.64), channel_id=1, source_target_pairs={{8,0},{9,1},{10,2},{11,3},{12,4},{13,5},{14,6},{15,7},{0,8},{1,9},... | collective-permute-start | bytes 675848 | tf_op jit(solution)/shard_map/ppermute | solution.py:46
  100.9 17.2 %collective-permute-done.21.refs_1_ = bf16[832,640]{1,0:T(8,128)(2,1)S(1)} collective-permute-done((bf16[832,640]{1,0:T(8,128)(2,1)S(1)}, bf16[832,640]{1,0:T(8,128)(2,1)S(1)}, u32[]{:S(2)}, u32[]{:S(2)}) %collective-permute-start.21) | collective-permute-done | bytes 1064992 | tf_op jit(solution)/shard_map/ppermute | solution.py:50
  118.1 0.6 shard_map.118
  118.8 1.2 collective-permute-done.26.refs_5_
  120.0 1.1 collective-permute-start.27
  121.1 2.5 %shard_map.120.refs_1_ = bf16[384,2560]{1,0:T(8,128)(2,1)} custom-call(s32[16]{0:T(128)S(1)} %copy-done.5, bf16[832,640]{1,0:T(8,128)(2,1)S(1)} %constant_dynamic-update-slice_fusion.4.refs_0_, bf16[832,640]{1,0:T(8,128)(2,1)S(1)} %collective-permute-done.21.refs_1_, bf16[176,640]{1,0:T(8,128)(2,1)S(1)} %get-tuple-element.67.refs_2_, ...), custom_call_target="tpu_custom_call" | custom-call | flops 1 | bytes 16384 | tf_op jit(solution)/shard_map/pallas_call | solution.py:281
  123.5 0.6 shard_map.121
  (42 shorter events, 1.3 us)
Async XLA Ops:
  1.9 1.1 copy-start.3
  3.0 0.9 copy-start.4
  4.1 7.5 %collective-permute-start.1 = (bf16[1072,128]{1,0:T(8,128)(2,1)S(1)}, bf16[1072,128]{1,0:T(8,128)(2,1)S(1)}, u32[]{:S(2)}, u32[]{:S(2)}) collective-permute-start(bf16[1072,128]{1,0:T(8,128)(2,1)S(1)} %get-tuple-element.37), channel_id=1, source_target_pairs={{12,0},{13,1},{14,2},{15,3},{0,4},{1,5},{2,6},{3,7},{4,8},{5,9},{6... | collective-permute-start | bytes 823304 | tf_op jit(solution)/shard_map/ppermute | solution.py:46
  5.5 13.9 %collective-permute-start.2 = (bf16[1072,128]{1,0:T(8,128)(2,1)S(1)}, bf16[1072,128]{1,0:T(8,128)(2,1)S(1)}, u32[]{:S(2)}, u32[]{:S(2)}) collective-permute-start(bf16[1072,128]{1,0:T(8,128)(2,1)S(1)} %get-tuple-element.38), channel_id=1, source_target_pairs={{4,0},{5,1},{6,2},{7,3},{8,4},{9,5},{10,6},{11,7},{12,8},{13,9},{1... | collective-permute-start | bytes 823304 | tf_op jit(solution)/shard_map/ppermute | solution.py:46
  5.6 13.8 %collective-permute-start = (bf16[1072,128]{1,0:T(8,128)(2,1)S(1)}, bf16[1072,128]{1,0:T(8,128)(2,1)S(1)}, u32[]{:S(2)}, u32[]{:S(2)}) collective-permute-start(bf16[1072,128]{1,0:T(8,128)(2,1)S(1)} %get-tuple-element.36.refs_0_), channel_id=1, source_target_pairs={{2,0},{3,1},{0,2},{1,3},{6,4},{7,5},{4,6},{5,7},{10,8},{11,9},{8,1... | collective-permute-start | bytes 823304 | tf_op jit(solution)/shard_map/ppermute | solution.py:50
  19.4 12.1 %collective-permute-start.4 = (bf16[1072,128]{1,0:T(8,128)(2,1)S(1)}, bf16[1072,128]{1,0:T(8,128)(2,1)S(1)}, u32[]{:S(2)}, u32[]{:S(2)}) collective-permute-start(bf16[1072,128]{1,0:T(8,128)(2,1)S(1)} %get-tuple-element.41), channel_id=1, source_target_pairs={{8,0},{9,1},{10,2},{11,3},{12,4},{13,5},{14,6},{15,7},{0,8},{1,9},... | collective-permute-start | bytes 823304 | tf_op jit(solution)/shard_map/ppermute | solution.py:46
  19.6 13.8 %collective-permute-start.6 = (bf16[2144,128]{1,0:T(8,128)(2,1)S(1)}, bf16[2144,128]{1,0:T(8,128)(2,1)S(1)}, u32[]{:S(2)}, u32[]{:S(2)}) collective-permute-start(bf16[2144,128]{1,0:T(8,128)(2,1)S(1)} %pad_maximum_fusion.2), channel_id=1, source_target_pairs={{2,0},{3,1},{0,2},{1,3},{6,4},{7,5},{4,6},{5,7},{10,8},{11,9},{8,1... | collective-permute-start | bytes 1646600 | tf_op jit(solution)/shard_map/ppermute | solution.py:50
  31.4 2.0 %collective-permute-start.5 = (bf16[1072,128]{1,0:T(8,128)(2,1)S(1)}, bf16[1072,128]{1,0:T(8,128)(2,1)S(1)}, u32[]{:S(2)}, u32[]{:S(2)}) collective-permute-start(bf16[1072,128]{1,0:T(8,128)(2,1)S(1)} %collective-permute-done.4.refs_5_), channel_id=1, source_target_pairs={{1,0},{0,1},{3,2},{2,3},{5,4},{4,5},{7,6},{6,7},{9,8},{8,9},{11,10... | collective-permute-start | bytes 823304 | tf_op jit(solution)/shard_map/ppermute | solution.py:50
  32.3 8.2 %collective-permute-start.7 = (bf16[1072,128]{1,0:T(8,128)(2,1)S(1)}, bf16[1072,128]{1,0:T(8,128)(2,1)S(1)}, u32[]{:S(2)}, u32[]{:S(2)}) collective-permute-start(bf16[1072,128]{1,0:T(8,128)(2,1)S(1)} %collective-permute-done.4.refs_5_), channel_id=1, source_target_pairs={{2,0},{3,1},{0,2},{1,3},{6,4},{7,5},{4,6},{5,7},{10,8},{11,9},{8,1... | collective-permute-start | bytes 823304 | tf_op jit(solution)/shard_map/ppermute | solution.py:50
  33.5 7.0 %collective-permute-start.8 = (bf16[352,128]{1,0:T(8,128)(2,1)S(1)}, bf16[352,128]{1,0:T(8,128)(2,1)S(1)}, u32[]{:S(2)}, u32[]{:S(2)}) collective-permute-start(bf16[352,128]{1,0:T(8,128)(2,1)S(1)} %get-tuple-element.43), channel_id=1, source_target_pairs={{12,0},{13,1},{14,2},{15,3},{0,4},{1,5},{2,6},{3,7},{4,8},{5,9},{6... | collective-permute-start | bytes 270344 | tf_op jit(solution)/shard_map/ppermute | solution.py:46
  34.4 9.8 %collective-permute-start.9 = (bf16[352,128]{1,0:T(8,128)(2,1)S(1)}, bf16[352,128]{1,0:T(8,128)(2,1)S(1)}, u32[]{:S(2)}, u32[]{:S(2)}) collective-permute-start(bf16[352,128]{1,0:T(8,128)(2,1)S(1)} %get-tuple-element.43), channel_id=1, source_target_pairs={{8,0},{9,1},{10,2},{11,3},{12,4},{13,5},{14,6},{15,7},{0,8},{1,9},... | collective-permute-start | bytes 270344 | tf_op jit(solution)/shard_map/ppermute | solution.py:46
  38.4 7.4 %collective-permute-start.10 = (bf16[352,128]{1,0:T(8,128)(2,1)S(1)}, bf16[352,128]{1,0:T(8,128)(2,1)S(1)}, u32[]{:S(2)}, u32[]{:S(2)}) collective-permute-start(bf16[352,128]{1,0:T(8,128)(2,1)S(1)} %get-tuple-element.43), channel_id=1, source_target_pairs={{4,0},{5,1},{6,2},{7,3},{8,4},{9,5},{10,6},{11,7},{12,8},{13,9},{1... | collective-permute-start | bytes 270344 | tf_op jit(solution)/shard_map/ppermute | solution.py:46
  38.5 10.5 %copy-start.5 = (s32[16]{0:T(128)S(1)}, s32[16]{0:T(128)}, u32[]{:S(2)}) copy-start(s32[16]{0:T(128)} %plan_ref.11) | copy-start | bytes 196
  38.5 9.8 %collective-permute-start.3 = (bf16[4288,128]{1,0:T(8,128)(2,1)S(1)}, bf16[4288,128]{1,0:T(8,128)(2,1)S(1)}, u32[]{:S(2)}, u32[]{:S(2)}) collective-permute-start(bf16[4288,128]{1,0:T(8,128)(2,1)S(1)} %pad_maximum_fusion), channel_id=1, source_target_pairs={{1,0},{0,1},{3,2},{2,3},{5,4},{4,5},{7,6},{6,7},{9,8},{8,9},{11,10... | collective-permute-start | bytes 3293192 | tf_op jit(solution)/shard_map/ppermute | solution.py:50
  45.9 3.2 %collective-permute-start.11 = (bf16[3216,128]{1,0:T(8,128)(2,1)S(1)}, bf16[3216,128]{1,0:T(8,128)(2,1)S(1)}, u32[]{:S(2)}, u32[]{:S(2)}) collective-permute-start(bf16[3216,128]{1,0:T(8,128)(2,1)S(1)} %pad_maximum_fusion.1), channel_id=1, source_target_pairs={{1,0},{0,1},{3,2},{2,3},{5,4},{4,5},{7,6},{6,7},{9,8},{8,9},{11,10... | collective-permute-start | bytes 2469896 | tf_op jit(solution)/shard_map/ppermute | solution.py:50
  47.2 10.1 %collective-permute-start.13 = (bf16[1408,128]{1,0:T(8,128)(2,1)S(1)}, bf16[1408,128]{1,0:T(8,128)(2,1)S(1)}, u32[]{:S(2)}, u32[]{:S(2)}) collective-permute-start(bf16[1408,128]{1,0:T(8,128)(2,1)S(1)} %constant_dynamic-update-slice_fusion.refs_10_), channel_id=1, source_target_pairs={{2,0},{3,1},{0,2},{1,3},{6,4},{7,5},{4,6},{5,7},{10,8},{11,9},{8,1... | collective-permute-start | bytes 1081352 | tf_op jit(solution)/shard_map/ppermute | solution.py:50
  50.6 13.6 %collective-permute-start.15 = (f32[208,640]{1,0:T(8,128)S(1)}, f32[208,640]{1,0:T(8,128)S(1)}, u32[]{:S(2)}, u32[]{:S(2)}) collective-permute-start(f32[208,640]{1,0:T(8,128)S(1)} %shard_map.112), channel_id=1, source_target_pairs={{16,0},{0,16},{17,1},{1,17},{18,2},{2,18},{19,3},{3,19},{20,4},{4,... | collective-permute-start | bytes 1597448 | tf_op jit(solution)/shard_map/ppermute | solution.py:46
  51.4 8.1 %collective-permute-start.12 = (bf16[1408,128]{1,0:T(8,128)(2,1)S(1)}, bf16[1408,128]{1,0:T(8,128)(2,1)S(1)}, u32[]{:S(2)}, u32[]{:S(2)}) collective-permute-start(bf16[1408,128]{1,0:T(8,128)(2,1)S(1)} %constant_dynamic-update-slice_fusion.refs_10_), channel_id=1, source_target_pairs={{1,0},{0,1},{3,2},{2,3},{5,4},{4,5},{7,6},{6,7},{9,8},{8,9},{11,10... | collective-permute-start | bytes 1081352 | tf_op jit(solution)/shard_map/ppermute | solution.py:50
  57.2 2.3 %collective-permute-start.14 = (bf16[1408,128]{1,0:T(8,128)(2,1)S(1)}, bf16[1408,128]{1,0:T(8,128)(2,1)S(1)}, u32[]{:S(2)}, u32[]{:S(2)}) collective-permute-start(bf16[1408,128]{1,0:T(8,128)(2,1)S(1)} %collective-permute-done.13.refs_12_), channel_id=1, source_target_pairs={{1,0},{0,1},{3,2},{2,3},{5,4},{4,5},{7,6},{6,7},{9,8},{8,9},{11,10... | collective-permute-start | bytes 1081352 | tf_op jit(solution)/shard_map/ppermute | solution.py:50
  61.1 3.2 %copy-start = (f32[1,384,640]{2,1,0:T(8,128)S(1)}, f32[1,384,640]{2,1,0:T(8,128)}, u32[]{:S(2)}) copy-start(f32[1,384,640]{2,1,0:T(8,128)} %param.13) | copy-start | bytes 2949124
  61.1 3.1 %copy-start.1 = (f32[1,384,640]{2,1,0:T(8,128)S(1)}, f32[1,384,640]{2,1,0:T(8,128)}, u32[]{:S(2)}) copy-start(f32[1,384,640]{2,1,0:T(8,128)} %param.14) | copy-start | bytes 2949124
  61.1 3.1 %copy-start.2 = (f32[1,384,640]{2,1,0:T(8,128)S(1)}, f32[1,384,640]{2,1,0:T(8,128)}, u32[]{:S(2)}) copy-start(f32[1,384,640]{2,1,0:T(8,128)} %param.15) | copy-start | bytes 2949124
  64.2 10.9 %collective-permute-start.16 = (f32[176,640]{1,0:T(8,128)S(1)}, f32[176,640]{1,0:T(8,128)S(1)}, u32[]{:S(2)}, u32[]{:S(2)}) collective-permute-start(f32[176,640]{1,0:T(8,128)S(1)} %shard_map.114), channel_id=1, source_target_pairs={{16,0},{0,16},{17,1},{1,17},{18,2},{2,18},{19,3},{3,19},{20,4},{4,... | collective-permute-start | bytes 1351688 | tf_op jit(solution)/shard_map/ppermute | solution.py:46
  65.6 14.3 %collective-permute-start.20 = (bf16[208,640]{1,0:T(8,128)(2,1)S(1)}, bf16[208,640]{1,0:T(8,128)(2,1)S(1)}, u32[]{:S(2)}, u32[]{:S(2)}) collective-permute-start(bf16[208,640]{1,0:T(8,128)(2,1)S(1)} %get-tuple-element.50), channel_id=1, source_target_pairs={{4,0},{5,1},{6,2},{7,3},{8,4},{9,5},{10,6},{11,7},{12,8},{13,9},{1... | collective-permute-start | bytes 798728 | tf_op jit(solution)/shard_map/ppermute | solution.py:46
  65.7 19.9 %collective-permute-start.19 = (bf16[208,640]{1,0:T(8,128)(2,1)S(1)}, bf16[208,640]{1,0:T(8,128)(2,1)S(1)}, u32[]{:S(2)}, u32[]{:S(2)}) collective-permute-start(bf16[208,640]{1,0:T(8,128)(2,1)S(1)} %get-tuple-element.50), channel_id=1, source_target_pairs={{8,0},{9,1},{10,2},{11,3},{12,4},{13,5},{14,6},{15,7},{0,8},{1,9},... | collective-permute-start | bytes 798728 | tf_op jit(solution)/shard_map/ppermute | solution.py:46
  66.6 22.4 %collective-permute-start.17 = (bf16[208,640]{1,0:T(8,128)(2,1)S(1)}, bf16[208,640]{1,0:T(8,128)(2,1)S(1)}, u32[]{:S(2)}, u32[]{:S(2)}) collective-permute-start(bf16[208,640]{1,0:T(8,128)(2,1)S(1)} %get-tuple-element.50), channel_id=1, source_target_pairs={{12,0},{13,1},{14,2},{15,3},{0,4},{1,5},{2,6},{3,7},{4,8},{5,9},{6... | collective-permute-start | bytes 798728 | tf_op jit(solution)/shard_map/ppermute | solution.py:46
  76.4 9.2 %collective-permute-start.18 = (bf16[176,640]{1,0:T(8,128)(2,1)S(1)}, bf16[176,640]{1,0:T(8,128)(2,1)S(1)}, u32[]{:S(2)}, u32[]{:S(2)}) collective-permute-start(bf16[176,640]{1,0:T(8,128)(2,1)S(1)} %get-tuple-element.58.refs_0_), channel_id=1, source_target_pairs={{2,0},{3,1},{0,2},{1,3},{6,4},{7,5},{4,6},{5,7},{10,8},{11,9},{8,1... | collective-permute-start | bytes 675848 | tf_op jit(solution)/shard_map/ppermute | solution.py:50
  89.1 29.0 %collective-permute-start.21 = (bf16[832,640]{1,0:T(8,128)(2,1)S(1)}, bf16[832,640]{1,0:T(8,128)(2,1)S(1)}, u32[]{:S(2)}, u32[]{:S(2)}) collective-permute-start(bf16[832,640]{1,0:T(8,128)(2,1)S(1)} %constant_dynamic-update-slice_fusion.4.refs_0_), channel_id=1, source_target_pairs={{2,0},{3,1},{0,2},{1,3},{6,4},{7,5},{4,6},{5,7},{10,8},{11,9},{8,1... | collective-permute-start | bytes 3194888 | tf_op jit(solution)/shard_map/ppermute | solution.py:50
  94.2 1.5 %collective-permute-start.22 = (bf16[176,640]{1,0:T(8,128)(2,1)S(1)}, bf16[176,640]{1,0:T(8,128)(2,1)S(1)}, u32[]{:S(2)}, u32[]{:S(2)}) collective-permute-start(bf16[176,640]{1,0:T(8,128)(2,1)S(1)} %get-tuple-element.58.refs_0_), channel_id=1, source_target_pairs={{1,0},{0,1},{3,2},{2,3},{5,4},{4,5},{7,6},{6,7},{9,8},{8,9},{11,10... | collective-permute-start | bytes 675848 | tf_op jit(solution)/shard_map/ppermute | solution.py:50
  94.2 1.8 %collective-permute-start.23 = (bf16[176,640]{1,0:T(8,128)(2,1)S(1)}, bf16[176,640]{1,0:T(8,128)(2,1)S(1)}, u32[]{:S(2)}, u32[]{:S(2)}) collective-permute-start(bf16[176,640]{1,0:T(8,128)(2,1)S(1)} %collective-permute-done.18.refs_2_), channel_id=1, source_target_pairs={{1,0},{0,1},{3,2},{2,3},{5,4},{4,5},{7,6},{6,7},{9,8},{8,9},{11,10... | collective-permute-start | bytes 675848 | tf_op jit(solution)/shard_map/ppermute | solution.py:50
  96.7 22.1 %collective-permute-start.24 = (bf16[176,640]{1,0:T(8,128)(2,1)S(1)}, bf16[176,640]{1,0:T(8,128)(2,1)S(1)}, u32[]{:S(2)}, u32[]{:S(2)}) collective-permute-start(bf16[176,640]{1,0:T(8,128)(2,1)S(1)} %get-tuple-element.63), channel_id=1, source_target_pairs={{12,0},{13,1},{14,2},{15,3},{0,4},{1,5},{2,6},{3,7},{4,8},{5,9},{6... | collective-permute-start | bytes 675848 | tf_op jit(solution)/shard_map/ppermute | solution.py:46
  98.6 20.1 %collective-permute-start.25 = (bf16[176,640]{1,0:T(8,128)(2,1)S(1)}, bf16[176,640]{1,0:T(8,128)(2,1)S(1)}, u32[]{:S(2)}, u32[]{:S(2)}) collective-permute-start(bf16[176,640]{1,0:T(8,128)(2,1)S(1)} %get-tuple-element.64), channel_id=1, source_target_pairs={{8,0},{9,1},{10,2},{11,3},{12,4},{13,5},{14,6},{15,7},{0,8},{1,9},... | collective-permute-start | bytes 675848 | tf_op jit(solution)/shard_map/ppermute | solution.py:46
  100.9 19.1 %collective-permute-start.26 = (bf16[176,640]{1,0:T(8,128)(2,1)S(1)}, bf16[176,640]{1,0:T(8,128)(2,1)S(1)}, u32[]{:S(2)}, u32[]{:S(2)}) collective-permute-start(bf16[176,640]{1,0:T(8,128)(2,1)S(1)} %get-tuple-element.65), channel_id=1, source_target_pairs={{4,0},{5,1},{6,2},{7,3},{8,4},{9,5},{10,6},{11,7},{12,8},{13,9},{1... | collective-permute-start | bytes 675848 | tf_op jit(solution)/shard_map/ppermute | solution.py:46
  120.0 3.5 %collective-permute-start.27 = (bf16[4,208,640]{2,1,0:T(8,128)(2,1)S(1)}, bf16[4,208,640]{2,1,0:T(8,128)(2,1)S(1)}, u32[]{:S(2)}, u32[]{:S(2)}) collective-permute-start(bf16[4,208,640]{2,1,0:T(8,128)(2,1)S(1)} %shard_map.118), channel_id=1, source_target_pairs={{1,0},{0,1},{3,2},{2,3},{5,4},{4,5},{7,6},{6,7},{9,8},{8,9},{11,10... | collective-permute-start | bytes 3194888 | tf_op jit(solution)/shard_map/ppermute | solution.py:50
